TPU v7x, 512 devices: a whole 4x8x8 slice. The times are simulated.
512 devices in a mesh: group: 16 (over y, core), dev: 32 (over z, x).
Axes of the slice: x: 4, y: 8, z: 8, core: 2. Of those that a mesh axis runs over, the one named last changes fastest.
Arguments:
- positions: float32 [3, 262144], P(None, ('group', 'dev')), may hold values from -5 to 14, as said below
- strengths: float32 [3, 262144], P(None, ('group', 'dev')), may hold values from -4 to 4
- pair_list: int32 [2, 3072], P(None, ('group', 'dev')), may hold values from 0 to 63, as said below
- pair_count: int32 [512], P(('group', 'dev')), may hold values from 1 to 6, as said below
- far_list: int32 [64, 1024], P(None, ('group', 'dev')), may hold values from 0 to 1023, as said below
Outputs:
- new_positions: float32 [3, 262144], P(None, ('group', 'dev'))
- new_strengths: float32 [3, 262144], P(None, ('group', 'dev'))
Inputs may be any that keep to these rules, and one draw needn't show every extreme that they name: `positions`: region g is centred at (3 (g mod 4), 3 ((g div 4) mod 4), 0); every particle lies within 5 of its region's centre in each component. `pair_list`: block numbers within a region; the two blocks of a slot differ. Slots at or beyond the device's count hold arbitrary block numbers of the same range. `pair_count`: some device has all 6 slots live in every draw. `far_list`: every listed cluster lies in another region than the block.
All inputs are finite; a program needn't handle non-finite values.
Results may differ from a plain program's by a relative error of at most 0.0003.
Values sent between devices are 32-bit elements; how exact they have to be, the bound alone decides.
No kernel may reach another device: no remote copies, remote signals or barrier semaphores. Data moves between devices by JAX's collectives and lax.ppermute only.
A program may use at most 64 MiB of HBM per device.

v0:
```python
import jax
import jax.numpy as jnp
from jax import lax
from jax.sharding import PartitionSpec as P

BS = 256
STEPS = 2


INV_FOUR_PI = 0.07957747154594767
CORE_SQUARED = 0.25
TIME_STEP = 0.05


def cross_stack(left, right):
    return jnp.stack(
        [
            left[1] * right[2] - left[2] * right[1],
            left[2] * right[0] - left[0] * right[2],
            left[0] * right[1] - left[1] * right[0],
        ]
    )


def one_sided(target_pos, target_str, source_pos, source_str):
    offset = target_pos[:, :, None] - source_pos[:, None, :]
    dist_sq = jnp.sum(offset * offset, axis=0) + CORE_SQUARED
    inv_root = lax.rsqrt(dist_sq)
    first_kernel = inv_root * inv_root * inv_root
    second_kernel = first_kernel * inv_root * inv_root
    source_b = source_str[:, None, :]
    target_a = target_str[:, :, None]
    spin = cross_stack(offset, source_b)
    twist = cross_stack(target_a, source_b)
    align = jnp.sum(target_a * offset, axis=0)
    velocity = -INV_FOUR_PI * jnp.sum(first_kernel * spin, axis=2)
    stretch = -INV_FOUR_PI * jnp.sum(
        first_kernel * twist - 3.0 * second_kernel * align * spin, axis=2
    )
    return jnp.concatenate([velocity, stretch], axis=0)


def both_sided(pos_first, str_first, pos_second, str_second):
    offset = pos_first[:, :, None] - pos_second[:, None, :]
    dist_sq = jnp.sum(offset * offset, axis=0) + CORE_SQUARED
    inv_root = lax.rsqrt(dist_sq)
    first_kernel = inv_root * inv_root * inv_root
    second_kernel = first_kernel * inv_root * inv_root
    first_str = str_first[:, :, None]
    second_str = str_second[:, None, :]
    spin_second = cross_stack(offset, second_str)
    spin_first = cross_stack(offset, first_str)
    twist = cross_stack(first_str, second_str)
    align_first = jnp.sum(first_str * offset, axis=0)
    align_second = jnp.sum(second_str * offset, axis=0)
    vel_first = -INV_FOUR_PI * jnp.sum(first_kernel * spin_second, axis=2)
    str_out_first = -INV_FOUR_PI * jnp.sum(
        first_kernel * twist - 3.0 * second_kernel * align_first * spin_second, axis=2
    )
    vel_second = INV_FOUR_PI * jnp.sum(first_kernel * spin_first, axis=1)
    str_out_second = -INV_FOUR_PI * jnp.sum(
        -first_kernel * twist - 3.0 * second_kernel * align_second * spin_first, axis=1
    )
    return (
        jnp.concatenate([vel_first, str_out_first], axis=0),
        jnp.concatenate([vel_second, str_out_second], axis=0),
    )


def body(positions, strengths, pair_list, pair_count, far_list):
    block_size = BS
    blocks_own = positions.shape[1] // block_size
    dev_count = lax.axis_size("dev")
    region_blocks = blocks_own * dev_count
    per_device = pair_list.shape[1]
    order = jnp.arange(per_device, dtype=jnp.int32)
    begin = jnp.int32(0)
    finish = pair_count[0]
    for advance in range(STEPS):
        state = jnp.concatenate([positions, strengths], axis=0)
        region_state = lax.all_gather(state, "dev", axis=1, tiled=True)
        own_state = state.reshape(6, blocks_own, block_size)
        centres = jnp.mean(own_state[:3], axis=2)
        totals = jnp.sum(own_state[3:], axis=2)
        all_moments = lax.all_gather(
            jnp.concatenate([centres, totals], axis=0), ("group", "dev"), axis=1, tiled=True
        )

        def visit(counter, accum):
            slot = order[counter]
            first = pair_list[0, slot]
            second = pair_list[1, slot]
            block_first = lax.dynamic_slice_in_dim(region_state, first * block_size, block_size, 1)
            block_second = lax.dynamic_slice_in_dim(
                region_state, second * block_size, block_size, 1
            )
            term_first, term_second = both_sided(
                block_first[:3], block_first[3:], block_second[:3], block_second[3:]
            )
            accum = accum.at[first].add(term_first)
            return accum.at[second].add(term_second)

        accum = jnp.zeros((region_blocks, 6, block_size), jnp.float32)
        accum = lax.fori_loop(begin, finish, visit, accum)
        near_terms = lax.psum_scatter(accum, "dev", scatter_dimension=0, tiled=True)

        def own_terms(index):
            block = lax.dynamic_index_in_dim(own_state, index, 1, keepdims=False)
            self_part = one_sided(block[:3], block[3:], block[:3], block[3:])
            far = jnp.take(all_moments, far_list[:, index], axis=1)
            far_part = one_sided(block[:3], block[3:], far[:3], far[3:])
            return (self_part, far_part)

        self_terms, far_terms = lax.map(own_terms, jnp.arange(blocks_own, dtype=jnp.int32))
        rates = near_terms + self_terms + far_terms
        rates = jnp.transpose(rates, (1, 0, 2)).reshape(6, blocks_own * block_size)
        positions = positions + TIME_STEP * rates[:3]
        strengths = strengths + TIME_STEP * rates[3:]
    return (positions, strengths)


def solution(mesh):
    return jax.shard_map(
        body,
        mesh=mesh,
        in_specs=(
            P(None, ("group", "dev")),
            P(None, ("group", "dev")),
            P(None, ("group", "dev")),
            P(("group", "dev")),
            P(None, ("group", "dev")),
        ),
        out_specs=(P(None, ("group", "dev")), P(None, ("group", "dev"))),
        check_vma=False,
    )
```

profile of v0, /device:TPU:1, one launch (start us, length us, event | category | flops | bytes accessed | tf_op | source)
XLA Modules:
  0.0 795.3 jit_solution(4147878623478451947)
XLA Ops:
  7.2 0.7 pad_maximum_fusion.10
  7.9 44.3 %all_gather.12 = f32[6,16384]{1,0:T(8,128)S(1)} all-gather(f32[6,512]{1,0:T(8,128)S(1)} %pad_maximum_fusion.10), channel_id=1, replica_groups=mesh['group'=16,'dev'=32] {'dev'}, dimensions={1}, use_global_device_ids=true | all-gather | bytes 405504 | tf_op jit(solution)/shard_map/all_gather | solution.py:81
  52.3 0.6 copy-done.2
  52.9 36.8 %while.48 = (s32[]{:T(128)}, f32[64,6,256]{2,1,0:T(8,128)S(1)}, s32[]{:T(128)}, s32[6]{0:T(128)S(1)}, s32[2,6]{1,0:T(2,128)S(1)}, /*index=5*/f32[6,16384]{1,0:T(...) while((s32[]{:T(128)}, f32[64,6,256]{2,1,0:T(8,128)S(1)}, ...), condition=%wide.region_10.11_spmd, body=%wide.region_0.10_spmd.sunk | while | flops 7087163 | bytes 10103313 | solution.py:104
  53.6 0.6 dynamic_slice.73
  56.1 0.6 constant_dynamic-slice_fusion.20
  60.5 0.6 multiply_reduce_fusion.26
  63.0 0.7 and_reduce_fusion.6
  63.8 0.6 fusion.66
  64.4 0.6 fusion.67
  65.7 0.6 dynamic_slice.73
  68.2 0.6 constant_dynamic-slice_fusion.20
  72.5 0.6 multiply_reduce_fusion.26
  75.1 0.7 and_reduce_fusion.6
  75.8 0.6 fusion.66
  76.5 0.6 fusion.67
  77.7 0.6 dynamic_slice.73
  80.2 0.6 constant_dynamic-slice_fusion.20
  84.6 0.6 multiply_reduce_fusion.26
  87.1 0.7 and_reduce_fusion.6
  87.9 0.6 fusion.66
  88.5 0.6 fusion.67
  89.8 0.8 copy-done
  90.6 0.6 copy-done.3
  91.7 145.7 %all-gather = f32[512,2,6]{2,1,0:T(2,128)S(1)} all-gather(f32[1,2,6]{2,1,0:T(2,128)S(1)} %maximum_bitcast_fusion.8), channel_id=1, replica_groups=mesh['group'=16,'dev'=32] {'group','dev'}, dimensions={0}, use_global_device_ids=true | all-gather | bytes 24624 | tf_op jit(solution)/shard_map/all_gather | solution.py:85
  237.4 0.7 copy-done.6
  238.1 9.9 %while.49 = (s32[]{:T(128)}, f32[2,6,256]{2,1,0:T(8,128)S(1)}, f32[2,6,256]{2,1,0:T(8,128)S(1)}, s32[2]{0:T(128)S(1)}, f32[6,2,256]{2,0,1:T(8,128)S(1)}, /*index...) while((s32[]{:T(128)}, f32[2,6,256]{2,1,0:T(8,128)S(1)}, ...), condition=%wide.region_23.25_spmd, body=%wide.region_14.24_spmd.sunk | while | flops 5575432 | bytes 8645495 | solution.py:114
  238.1 0.6 dynamic_slice.74
  241.6 0.6 gather_fusion
  243.0 0.6 dynamic_slice.74
  246.6 0.6 gather_fusion
  248.0 101.6 %reduce-scatter.3.cloned.1.call-done = f32[2,6,256]{2,1,0:T(8,128)} async-done(((f32[64,6,256]{2,1,0:T(8,128)}), f32[2,6,256]{2,1,0:T(8,128)}) %reduce-scatter.3.cloned.1.call-update) | async-done | bytes 12304 | tf_op jit(solution)/shard_map/reduce_scatter | solution.py:105
  349.5 0.7 add_bitcast_fusion.1
  350.8 103.8 %all-gather.1 = f32[512,2,6]{2,1,0:T(2,128)S(1)} all-gather(f32[1,2,6]{2,1,0:T(2,128)S(1)} %maximum_bitcast_fusion.9), channel_id=1, replica_groups=mesh['group'=16,'dev'=32] {'group','dev'}, dimensions={0}, use_global_device_ids=true | all-gather | bytes 24624 | tf_op jit(solution)/shard_map/all_gather | solution.py:85
  454.6 36.1 %all_gather.14 = f32[6,16384]{1,0:T(8,128)S(1)} all-gather(f32[6,512]{1,0:T(8,128)S(1)} %pad_maximum_fusion.11), channel_id=1, replica_groups=mesh['group'=16,'dev'=32] {'dev'}, dimensions={1}, use_global_device_ids=true | all-gather | bytes 405504 | tf_op jit(solution)/shard_map/all_gather | solution.py:81
  490.8 37.7 %while.50 = (s32[]{:T(128)}, f32[64,6,256]{2,1,0:T(8,128)S(1)}, s32[]{:T(128)}, s32[6]{0:T(128)S(1)}, s32[2,6]{1,0:T(2,128)S(1)}, /*index=5*/f32[6,16384]{1,0:T(...) while((s32[]{:T(128)}, f32[64,6,256]{2,1,0:T(8,128)S(1)}, ...), condition=%wide.region_34.36_spmd, body=%wide.region_24.35_spmd.sunk | while | flops 7087163 | bytes 10103313 | solution.py:104
  491.4 0.7 dynamic_slice.76
  494.2 0.6 constant_dynamic-slice_fusion.22
  498.6 0.6 multiply_reduce_fusion.31
  501.0 0.8 and_reduce_fusion.7
  501.8 0.6 fusion.75
  502.5 0.6 fusion.76
  503.8 0.7 dynamic_slice.76
  506.5 0.6 constant_dynamic-slice_fusion.22
  510.9 0.6 multiply_reduce_fusion.31
  513.4 0.8 and_reduce_fusion.7
  514.2 0.6 fusion.75
  514.8 0.6 fusion.76
  516.1 0.7 dynamic_slice.76
  518.9 0.6 constant_dynamic-slice_fusion.22
  523.3 0.6 multiply_reduce_fusion.31
  525.7 0.8 and_reduce_fusion.7
  526.5 0.6 fusion.75
  527.2 0.6 fusion.76
  528.5 0.8 copy-done.1
  529.3 9.9 %while.51 = (s32[]{:T(128)}, f32[2,6,256]{2,1,0:T(8,128)S(1)}, f32[2,6,256]{2,1,0:T(8,128)S(1)}, s32[2]{0:T(128)S(1)}, f32[6,2,256]{2,0,1:T(8,128)S(1)}, /*index...) while((s32[]{:T(128)}, f32[2,6,256]{2,1,0:T(8,128)S(1)}, ...), condition=%wide.region_47.49_spmd, body=%wide.region_38.48_spmd.sunk | while | flops 5575432 | bytes 8645495 | solution.py:114
  529.3 0.6 dynamic_slice.77
  532.9 0.6 gather_fusion.1
  534.3 0.6 dynamic_slice.77
  537.9 0.6 gather_fusion.1
  539.2 247.3 %reduce-scatter.5.cloned.1.call-done = f32[2,6,256]{2,1,0:T(8,128)} async-done(((f32[64,6,256]{2,1,0:T(8,128)}), f32[2,6,256]{2,1,0:T(8,128)}) %reduce-scatter.5.cloned.1.call-update) | async-done | bytes 12304 | tf_op jit(solution)/shard_map/reduce_scatter | solution.py:105
  786.5 0.7 add_bitcast_fusion
  787.3 0.6 add.199
  787.9 0.6 add.200
  (166 shorter events, 13.1 us)
Async XLA Ops:
  7.2 342.4 %reduce-scatter.3.cloned.1.call-start = ((), (), s32[]{:S(2)}) async-start(), calls=%async_computation.2 | async-start | bytes 540672 | tf_op jit(solution)/shard_map/reduce_scatter | solution.py:105
  52.3 0.7 copy-start.2
  52.3 0.7 copy-start.5
  89.7 0.8 copy-start
  89.8 0.9 copy-start.4
  90.6 0.7 copy-start.3
  90.6 696.0 %reduce-scatter.5.cloned.1.call-start = ((), (), s32[]{:S(2)}) async-start(), calls=%async_computation.3 | async-start | bytes 540672 | tf_op jit(solution)/shard_map/reduce_scatter | solution.py:105
  237.4 0.7 copy-start.6
  528.5 0.8 copy-start.1
Sparse Core Ops, SparseCore 0:
  90.7 258.8 reduce-scatter.2
  529.4 257.0 reduce-scatter.4
where the time goes:
time: 802 us; the launch traced here: 795 us
  waiting for transfers between devices  349 us (44%)
  blocking collectives  330 us (41%)
  loops' own time  54.9 us (7%)
  other arithmetic  28.9 us (4%)
  local copies, waits for them, and re-layouts  18.4 us (2%)
  between operations  14.2 us (2%)
    reduce_scatter x2, waiting for transfers between devices, body(): near_terms = lax.psum_scatter(accum, 'dev', scatter_dimension=0, tiled=True)  349 us
    all_gather x2, blocking collectives, body(): lax.all_gather(jnp.concatenate([centres, totals], axis=0), ('group', 'dev...  249 us
    all_gather x2, blocking collectives, body(): region_state = lax.all_gather(state, 'dev', axis=1, tiled=True)  80.5 us
    another operation x2, loops' own time, body(): accum = lax.fori_loop(begin, finish, visit, accum)  46.6 us
  transfers between devices with their start and end apart: 2, of which 2 were waited for; matrix products, arithmetic and copies ran while one was open for 2% of the time, Pallas kernels for 0%

commit v1 on v0

v1 whole, which is shorter than its diff:
```python
import functools

import jax
import jax.numpy as jnp
from jax import lax
from jax.experimental import pallas as pl
from jax.experimental.pallas import tpu as pltpu
from jax.sharding import PartitionSpec as P

BS = 256
STEPS = 2
NZ, NX, NY, NC = 8, 4, 8, 2
N_DEV = NZ * NX
N_GROUP = NY * NC
REGION_BLOCKS = 2 * N_DEV
CHUNK = 32

INV_FOUR_PI = 0.07957747154594767
CORE_SQUARED = 0.25
TIME_STEP = 0.05

VMEM = pltpu.VMEM
SMEM = pltpu.SMEM


def split_rows(rows):
    high = rows.astype(jnp.bfloat16).astype(jnp.float32)
    rest = rows - high
    middle = rest.astype(jnp.bfloat16).astype(jnp.float32)
    parts = [high, middle, rest - middle, jnp.zeros_like(rows)]
    return jnp.concatenate(parts, axis=0).astype(jnp.bfloat16)


def fill_kernels(target, source, mats, count):
    tx, ty, tz = target[0:1], target[1:2], target[2:3]
    ax, ay, az = target[3:4], target[4:5], target[5:6]
    columns = source.T
    for start in range(0, count, CHUNK):
        part = columns[start : start + CHUNK]
        dx = tx - part[:, 0:1]
        dy = ty - part[:, 1:2]
        dz = tz - part[:, 2:3]
        dist_sq = dx * dx + dy * dy + dz * dz + CORE_SQUARED
        inv_root = lax.rsqrt(dist_sq)
        inv_sq = inv_root * inv_root
        first = inv_sq * inv_root
        align = ax * dx + ay * dy + az * dz
        second = first * inv_sq * align
        first_high = first.astype(jnp.bfloat16)
        second_high = second.astype(jnp.bfloat16)
        rows = pl.ds(start, CHUNK)
        mats[0, rows, :] = first_high
        mats[1, rows, :] = (first - first_high.astype(jnp.float32)).astype(jnp.bfloat16)
        mats[2, rows, :] = second_high
        mats[3, rows, :] = (second - second_high.astype(jnp.float32)).astype(jnp.bfloat16)


def weighted_sums(source, mats, count):
    yx, yy, yz = source[0:1], source[1:2], source[2:3]
    bx, by, bz = source[3:4], source[4:5], source[5:6]
    zero = jnp.zeros_like(yx)
    rows = jnp.concatenate(
        [bx, by, bz, yy * bz - yz * by, yz * bx - yx * bz, yx * by - yy * bx, zero, zero], axis=0
    )
    left = split_rows(rows)

    def product(high, low):
        top = jnp.dot(left, mats[high, 0:count, :], preferred_element_type=jnp.float32)
        rest = jnp.dot(left, mats[low, 0:count, :], preferred_element_type=jnp.float32)
        total = top + rest
        return total[0:8] + (total[8:16] + total[16:24])

    return jnp.concatenate([product(0, 1), product(2, 3)], axis=0)


def cross_rows(left, right):
    return jnp.concatenate(
        [
            left[1:2] * right[2:3] - left[2:3] * right[1:2],
            left[2:3] * right[0:1] - left[0:1] * right[2:3],
            left[0:1] * right[1:2] - left[1:2] * right[0:1],
        ],
        axis=0,
    )


def advance_rows(target, sums):
    position, strength = target[0:3], target[3:6]
    velocity = cross_rows(position, sums[0:3]) - sums[3:6]
    twist = cross_rows(strength, sums[0:3])
    spin = cross_rows(position, sums[8:11]) - sums[11:14]
    scale = -INV_FOUR_PI * TIME_STEP
    return scale * jnp.concatenate([velocity, twist - 3.0 * spin], axis=0)


STATE_LANES = 6 * 2 * BS
WIDTH = STATE_LANES + 128


def centre_of(state):
    row = lax.broadcasted_iota(jnp.int32, (8, BS), 0)
    mean = jnp.sum(state, axis=1, keepdims=True) * (1.0 / BS)
    return jnp.where(row < 3, jnp.broadcast_to(mean, (8, BS)), 0.0)


def publish(blocks, info, payload_ref, mine_ref):
    lane = lax.broadcasted_iota(jnp.int32, (8, 128), 1)
    row = lax.broadcasted_iota(jnp.int32, (8, 128), 0)
    table = jnp.zeros((8, 128), jnp.float32)
    for index, block in enumerate(blocks):
        total = jnp.sum(block, axis=1, keepdims=True)
        total = jnp.where(row < 3, total * (1.0 / BS), jnp.broadcast_to(total, (8, 128)))
        table = jnp.where(lane == 8 * index + row, total, table)
        mine_ref[index] = block
    tail = jnp.sum(table, axis=0, keepdims=True)
    if info is not None:
        tail = tail + info
    for device in range(8):
        for c in range(6):
            for index, block in enumerate(blocks):
                payload_ref[device, :, pl.ds(2 * BS * c + BS * index, BS)] = block[c : c + 1]
        payload_ref[device, :, pl.ds(STATE_LANES, 128)] = tail
    for device in range(8, N_DEV, 8):
        payload_ref[device : device + 8] = payload_ref[0:8]


def pack_kernel(pair_ref, count_ref, position_ref, strength_ref, far_ref, row_ref, *out_refs):
    row_ref[...] = jnp.concatenate([far_ref[0:1], far_ref[1:2]], axis=1)
    zero = jnp.zeros((2, 2 * BS), jnp.float32)
    state = jnp.concatenate([position_ref[...], strength_ref[...], zero], axis=0)
    lane = lax.broadcasted_iota(jnp.int32, (1, 128), 1)
    info = jnp.zeros((1, 128), jnp.int32)
    for side in range(2):
        for slot in range(6):
            info = jnp.where(lane == 16 + 6 * side + slot, pair_ref[side, slot], info)
    info = jnp.where(lane == 28, count_ref[0], info)
    publish([state[:, 0:BS], state[:, BS:]], info.astype(jnp.float32), *out_refs)


def visit_counts(base, info):
    lane = lax.broadcasted_iota(jnp.int32, (N_DEV, 128), 1)
    live = info[:, 28:29]
    counts = jnp.zeros((N_DEV, 128), jnp.int32)
    for slot in range(6):
        first = info[:, 16 + slot : 17 + slot]
        second = info[:, 22 + slot : 23 + slot]
        for target, source in ((first, second), (second, first)):
            own = target - base
            code = jnp.where((own >= 0) & (own < 2) & (slot < live), own * 64 + source, -1)
            counts = counts + jnp.where(lane == code, 1, 0)
    return jnp.sum(counts, axis=0, keepdims=True)


def moment_kernel(region_ref, moment_ref):
    columns = region_ref[:, 0, STATE_LANES:].T
    rows = [columns[8 * t + c : 8 * t + c + 1] for c in range(6) for t in range(2)]
    table = jnp.concatenate(rows, axis=1)
    for group in range(N_GROUP):
        moment_ref[group] = table


def self_kernel(mine_ref, *refs):
    if len(refs) == 2:
        out_ref, mats = refs
    else:
        me_ref, region_ref, out_ref, count_ref, mats = refs
        tails = region_ref[:, 0, STATE_LANES:]
        count_ref[...] = visit_counts(2 * me_ref[0], tails.astype(jnp.int32))
    for block in range(2):
        state = mine_ref[block]
        centre = centre_of(state)
        target = state - centre
        fill_kernels(target, target, mats.at[block], BS)
        out_ref[block, 0:16] = weighted_sums(target, mats.at[block], BS)
        out_ref[block, 16:24] = target
        out_ref[block, 24:32] = centre


def visit_list(count_ref, list_ref):
    def add(code, place):
        times = count_ref[0, code]
        list_ref[place] = times * 128 + code
        return place + jnp.where(times > 0, 1, 0)

    place = lax.fori_loop(0, 128, add, jnp.int32(1), unroll=16)
    list_ref[0] = place - 1


def near_kernel(count_ref, self_ref, region_ref, sum_ref, mats, list_ref):
    visit_list(count_ref, list_ref)
    sum_ref[...] = self_ref[:, 0:16]

    def visit(place, slot):
        code = list_ref[place]
        times = (code // 128).astype(jnp.float32)
        block = code // 64 % 2
        source = code % 64
        rows = []
        for c in range(6):
            lanes = pl.ds(pl.multiple_of(2 * BS * c + BS * (source % 2), BS), BS)
            rows.append(region_ref[source // 2, :, lanes])
        rows.append(jnp.zeros((2, BS), jnp.float32))
        rows = jnp.concatenate(rows, axis=0) - self_ref[block, 24:32]
        fill_kernels(self_ref[block, 16:24], rows, mats.at[slot], BS)
        return block, times * weighted_sums(rows, mats.at[slot], BS)

    def visit_two(index, carry):
        block_a, sums_a = visit(2 * index + 1, 0)
        block_b, sums_b = visit(2 * index + 2, 1)
        sum_ref[block_a] += sums_a
        sum_ref[block_b] += sums_b
        return carry

    count = list_ref[0]
    lax.fori_loop(0, count // 2, visit_two, 0)

    @pl.when(count % 2 == 1)
    def _():
        block, sums = visit(count, 0)
        sum_ref[block] += sums


def far_sources(far_ref, moment_ref):
    table = moment_ref[:, 0, :]
    table = jnp.concatenate(
        [table[:, REGION_BLOCKS * c : REGION_BLOCKS * c + REGION_BLOCKS] for c in range(6)], axis=0
    )
    size = table.shape[0]
    high = table.astype(jnp.bfloat16).astype(jnp.float32)
    middle = (table - high).astype(jnp.bfloat16).astype(jnp.float32)
    parts = jnp.concatenate([high, middle, table - high - middle], axis=0).astype(jnp.bfloat16)
    wanted = far_ref[...]
    place = wanted % 2 * N_DEV + wanted % REGION_BLOCKS // 2
    lanes = lax.broadcasted_iota(jnp.int32, (REGION_BLOCKS, 128), 0)
    chosen = jnp.where(lanes == place, 1.0, 0.0).astype(jnp.bfloat16)
    found = jnp.dot(parts, chosen, preferred_element_type=jnp.float32)
    found = found[0:size] + found[size : 2 * size] + found[2 * size :]
    groups = lax.broadcasted_iota(jnp.int32, (N_GROUP, 128), 0)
    mine = groups == wanted // REGION_BLOCKS
    rows = []
    for c in range(6):
        part = found[N_GROUP * c : N_GROUP * c + N_GROUP]
        rows.append(jnp.sum(jnp.where(mine, part, 0.0), axis=0, keepdims=True))
    return jnp.concatenate(rows + [jnp.zeros((2, 128), jnp.float32)], axis=0)


def far_kernel(last, far_ref, mine_ref, self_ref, sum_ref, moment_ref, *refs):
    *outs, mats = refs
    rows = far_sources(far_ref, moment_ref)
    blocks = []
    for block in range(2):
        target = self_ref[block, 16:24]
        source = rows[:, 64 * block : 64 * block + 64] - self_ref[block, 24:32][:, 0:64]
        fill_kernels(target, source, mats.at[block], 64)
        sums = sum_ref[block] + weighted_sums(source, mats.at[block], 64)
        new = mine_ref[block, 0:6] + advance_rows(target, sums)
        blocks.append(jnp.concatenate([new, jnp.zeros((2, BS), jnp.float32)], axis=0))
    if last:
        position_ref, strength_ref = outs
        state = jnp.concatenate(blocks, axis=1)
        position_ref[...] = state[0:3]
        strength_ref[...] = state[3:6]
    else:
        publish(blocks, None, *outs)


def f32(*shape):
    return jax.ShapeDtypeStruct(shape, jnp.float32)


def kept(*shape):
    return pltpu.VMEM(shape, jnp.float32)


def keep(value):
    return pltpu.with_memory_space_constraint(value, VMEM)


def in_vmem(count):
    return [pl.BlockSpec(memory_space=VMEM)] * count


def in_smem(count):
    return [pl.BlockSpec(memory_space=SMEM)] * count


PUBLISHED = (kept(N_DEV, 1, WIDTH), kept(2, 8, BS))


def pack(pair_list, pair_count, positions, strengths, far_list):
    return pl.pallas_call(
        pack_kernel,
        out_shape=(pltpu.VMEM((1, 128), jnp.int32),) + PUBLISHED,
        in_specs=in_smem(2) + in_vmem(3),
        out_specs=tuple(in_vmem(3)),
        name="pack",
    )(pair_list, pair_count, positions, strengths, far_list.T)


def moments_of(region):
    return pl.pallas_call(
        moment_kernel,
        out_shape=kept(N_GROUP, 1, 6 * REGION_BLOCKS),
        in_specs=in_vmem(1),
        out_specs=in_vmem(1)[0],
        name="moments",
    )(region)


def self_terms(mine, *pair_operands):
    out_shape, out_specs, in_specs = (kept(2, 32, BS),), in_vmem(1), in_vmem(1)
    if pair_operands:
        out_shape += (jax.ShapeDtypeStruct((1, 128), jnp.int32),)
        out_specs = in_vmem(2)
        in_specs = in_vmem(1) + in_smem(1) + in_vmem(1)
    return pl.pallas_call(
        self_kernel,
        out_shape=out_shape,
        in_specs=in_specs,
        out_specs=tuple(out_specs),
        scratch_shapes=[pltpu.VMEM((2, 4, BS, BS), jnp.bfloat16)],
        cost_estimate=pl.CostEstimate(flops=4000000, bytes_accessed=60000, transcendentals=130000),
        name="self_terms",
    )(keep(mine), *pair_operands)


def near(counts, own, region):
    return pl.pallas_call(
        near_kernel,
        out_shape=kept(2, 16, BS),
        in_specs=in_smem(1) + in_vmem(2),
        out_specs=in_vmem(1)[0],
        scratch_shapes=[pltpu.VMEM((2, 4, BS, BS), jnp.bfloat16), pltpu.SMEM((136,), jnp.int32)],
        cost_estimate=pl.CostEstimate(flops=20000000, bytes_accessed=600000, transcendentals=500000),
        name="near",
    )(counts, keep(own), region)


def far(far_row, mine, own, sums, moments, last):
    out_shape = (f32(3, 2 * BS), f32(3, 2 * BS)) if last else PUBLISHED
    return pl.pallas_call(
        functools.partial(far_kernel, last),
        out_shape=out_shape,
        in_specs=in_vmem(5),
        out_specs=tuple(in_vmem(len(out_shape))),
        scratch_shapes=[pltpu.VMEM((2, 4, 64, BS), jnp.bfloat16)],
        name="far",
    )(keep(far_row), keep(mine), keep(own), keep(sums), keep(moments))


def exchange(value, axis):
    return lax.all_to_all(value, axis, 0, 0, tiled=True)


def body(positions, strengths, pair_list, pair_count, far_list):
    me = lax.axis_index("dev").astype(jnp.int32).reshape(1)
    far_row, payload, mine = pack(pair_list, pair_count, positions, strengths, far_list)
    counts = None
    for step in range(STEPS):
        first, last = step == 0, step == STEPS - 1
        region = keep(exchange(payload, "dev"))
        moments = exchange(moments_of(region), "group")
        if first:
            own, counts = self_terms(mine, me, region)
        else:
            (own,) = self_terms(mine)
        sums = near(counts, own, region)
        result = far(far_row, mine, own, sums, moments, last)
        if not last:
            payload, mine = result
    return result


def solution(mesh):
    split = P(None, ("group", "dev"))
    return jax.shard_map(
        body,
        mesh=mesh,
        in_specs=(split, split, split, P(("group", "dev")), split),
        out_specs=(split, split),
        check_vma=False,
    )
```

time: 802 us -> 85.2 us (0.11)
  waiting for transfers between devices: 349 us -> 8.85 us
  blocking collectives: 330 us -> 45 us
  loops' own time: 54.9 us -> 0 us
  other arithmetic: 28.9 us -> 0 us
  starting transfers between devices: 0.08 us -> 19.1 us
  local copies, waits for them, and re-layouts: 18.4 us -> 0 us
  between operations: 14.2 us -> 1.31 us
  Pallas kernels: 0 us -> 10.5 us
    reduce_scatter x2 -> x0, waiting for transfers between devices: 349 us -> none  [body(): near_terms = lax.psum_scatter(accum, 'dev', scatter_dimension=0, tiled=True)]
    all_gather x4 -> x0, blocking collectives: 330 us -> none  [the longest x2 249 us: body(): lax.all_gather(jnp.concatenate([centres, totals], axis=0), ('group', 'dev...]
    another operation x4 -> x0, loops' own time: 54.9 us -> none  [the longest x2 46.6 us: body(): accum = lax.fori_loop(begin, finish, visit, accum)]
    all_to_all x0 -> x2, blocking collectives: none -> 45 us  [exchange(): return lax.all_to_all(value, axis, 0, 0, tiled=True)]
    all_to_all x0 -> x2, starting transfers between devices: none -> 19.1 us  [exchange(): return lax.all_to_all(value, axis, 0, 0, tiled=True)]
    pallas_call x0 -> x9, Pallas kernels: none -> 10.5 us  [the longest x2 3.74 us: self_terms(): pl.pallas_call(self_kernel, out_shape=out_shape, in_specs=in_specs, out_s...]
    dynamic_slice x16 -> x0, local copies, waits for them, and re-layouts: 9.7 us -> none  [the longest x6 3.76 us: visit(): slot = order[counter]]
    all_to_all x0 -> x2, waiting for transfers between devices: none -> 8.85 us  [exchange(): return lax.all_to_all(value, axis, 0, 0, tiled=True)]
  transfers between devices with their start and end apart: 2 -> 2, of which waited for: 2 -> 2; matrix products, arithmetic and copies ran while one was open for 2% -> 0% of each run, Pallas kernels for 0% -> 7%
where the time goes in v1:
time: 85.2 us; the launch traced here: 84.9 us
  blocking collectives  45 us (53%)
  starting transfers between devices  19.1 us (22%)
  Pallas kernels  10.5 us (12%)
  waiting for transfers between devices  8.85 us (10%)
  between operations  1.31 us (2%)
    all_to_all x2, blocking collectives, exchange(): return lax.all_to_all(value, axis, 0, 0, tiled=True)  45 us
    all_to_all x2, starting transfers between devices, exchange(): return lax.all_to_all(value, axis, 0, 0, tiled=True)  19.1 us
    all_to_all x2, waiting for transfers between devices, exchange(): return lax.all_to_all(value, axis, 0, 0, tiled=True)  8.85 us
    pallas_call x2, Pallas kernels, self_terms(): pl.pallas_call(self_kernel, out_shape=out_shape, in_specs=in_specs, out_s...  3.74 us
    pallas_call x2, Pallas kernels, far(): pl.pallas_call(functools.partial(far_kernel, last), out_shape=out_shape,...  2.24 us
    pallas_call x2, Pallas kernels, near(): pl.pallas_call(near_kernel, out_shape=kept(2, 16, BS), in_specs=in_smem(1...  2.08 us
  transfers between devices with their start and end apart: 2, of which 2 were waited for; matrix products, arithmetic and copies ran while one was open for 0% of the time, Pallas kernels for 7%

profile of v1, /device:TPU:1, one launch (start us, length us, event | category | flops | bytes accessed | tf_op | source)
XLA Modules:
  0.0 84.9 jit_solution(16217899005678316537)
XLA Ops:
  1.3 0.9 %pack.1 = (s32[1,128]{1,0:T(1,128)S(1)}, f32[32,1,3200]{2,1,0:T(1,128)S(1)}, f32[2,8,256]{2,1,0:T(8,128)S(1)}) custom-call(s32[2,6]{1,0:T(2,128)} %pair_ref.1, s32[1]{0:T(128)S(6)} %copy.7.count_ref, f32[3,512]{1,0:T(4,128)} %position_ref.1, f32[3,512]{1,0:T(4,128)} %strength_ref.1, s32[2,64]{1,0:T(2,128)} %bitcast.2), custom_call_target="tpu_custom_call" | custom-call | tf_op jit(solution)/shard_map/pack/pallas_call | solution.py:291
  2.2 27.2 %all_to_all.20.refs_1_.region_ref = f32[32,1,3200]{2,1,0:T(1,128)S(1)} all-to-all(f32[32,1,3200]{2,1,0:T(1,128)S(1)} %get-tuple-element.11), channel_id=1, replica_groups=mesh['group'=16,'dev'=32] {'dev'}, dimensions={0} | all-to-all | bytes 819200 | tf_op jit(solution)/shard_map/all_to_all | solution.py:352
  29.4 0.8 moments.2
  30.2 10.0 %all-to-all-start.1 = ((f32[16,1,384]{2,1,0:T(1,128)}), f32[16,1,384]{2,1,0:T(1,128)S(1)}, u32[]{:S(2)}, u32[]{:S(2)}) async-start(f32[16,1,384]{2,1,0:T(1,128)} %moments.2), calls=%async_computation.1 | async-start | bytes 49152 | tf_op jit(solution)/shard_map/all_to_all | solution.py:352
  40.2 2.8 %self_terms.2 = (f32[2,32,256]{2,1,0:T(8,128)S(1)}, s32[1,128]{1,0:T(1,128)}) custom-call(f32[2,8,256]{2,1,0:T(8,128)S(1)} %get-tuple-element.10.mine_ref, s32[1]{0:T(128)} %bitcast.1.refs_0_, f32[32,1,3200]{2,1,0:T(1,128)S(1)} %all_to_all.20.refs_1_.region_ref), custom_call_target="tpu_custom_call" | custom-call | flops 4000000 | bytes 60000 | tf_op jit(solution)/shard_map/self_terms/pallas_call | solution.py:316
  43.0 1.0 %near.2.sum_ref = f32[2,16,256]{2,1,0:T(8,128)S(1)} custom-call(s32[1,128]{1,0:T(1,128)} %get-tuple-element.13.count_ref, f32[2,32,256]{2,1,0:T(8,128)S(1)} %get-tuple-element.12.self_ref, f32[32,1,3200]{2,1,0:T(1,128)S(1)} %all_to_all.20.refs_1_.region_ref), custom_call_target="tpu_custom_call" | custom-call | flops 20000000 | bytes 600000 | tf_op jit(solution)/shard_map/near/pallas_call | solution.py:328
  44.1 3.5 %all-to-all-done.1.moment_ref = f32[16,1,384]{2,1,0:T(1,128)S(1)} async-done(((f32[16,1,384]{2,1,0:T(1,128)}), f32[16,1,384]{2,1,0:T(1,128)S(1)}, u32[]{:S(2)}, u32[]{:S(2)}) %all-to-all-start.1) | async-done | bytes 24608 | tf_op jit(solution)/shard_map/all_to_all | solution.py:352
  47.6 0.9 %far.2 = (f32[32,1,3200]{2,1,0:T(1,128)S(1)}, f32[2,8,256]{2,1,0:T(8,128)S(1)}) custom-call(s32[1,128]{1,0:T(1,128)S(1)} %get-tuple-element.9.far_ref, f32[2,8,256]{2,1,0:T(8,128)S(1)} %get-tuple-element.10.mine_ref, f32[2,32,256]{2,1,0:T(8,128)S(1)} %get-tuple-element.12.self_ref, f32[2,16,256]{2,1,0:T(8,128)S(1)} %near.2.sum_ref, ...), custom_call_target="tpu_custom_call" | custom-call | tf_op jit(solution)/shard_map/far/pallas_call | solution.py:341
  48.4 17.8 %all_to_all.21.region_ref = f32[32,1,3200]{2,1,0:T(1,128)S(1)} all-to-all(f32[32,1,3200]{2,1,0:T(1,128)S(1)} %get-tuple-element.15), channel_id=1, replica_groups=mesh['group'=16,'dev'=32] {'dev'}, dimensions={0} | all-to-all | bytes 819200 | tf_op jit(solution)/shard_map/all_to_all | solution.py:352
  66.3 0.8 moments.3
  67.0 9.1 %all-to-all-start.3 = ((f32[16,1,384]{2,1,0:T(1,128)}), f32[16,1,384]{2,1,0:T(1,128)S(1)}, u32[]{:S(2)}, u32[]{:S(2)}) async-start(f32[16,1,384]{2,1,0:T(1,128)} %moments.3), calls=%async_computation.3 | async-start | bytes 49152 | tf_op jit(solution)/shard_map/all_to_all | solution.py:352
  76.1 1.0 %self_terms.3.self_ref = f32[2,32,256]{2,1,0:T(8,128)S(1)} custom-call(f32[2,8,256]{2,1,0:T(8,128)S(1)} %get-tuple-element.14.mine_ref), custom_call_target="tpu_custom_call" | custom-call | flops 4000000 | bytes 60000 | tf_op jit(solution)/shard_map/self_terms/pallas_call | solution.py:316
  77.1 1.0 %near.3.sum_ref = f32[2,16,256]{2,1,0:T(8,128)S(1)} custom-call(s32[1,128]{1,0:T(1,128)} %get-tuple-element.13.count_ref, f32[2,32,256]{2,1,0:T(8,128)S(1)} %self_terms.3.self_ref, f32[32,1,3200]{2,1,0:T(1,128)S(1)} %all_to_all.21.region_ref), custom_call_target="tpu_custom_call" | custom-call | flops 20000000 | bytes 600000 | tf_op jit(solution)/shard_map/near/pallas_call | solution.py:328
  78.2 5.3 %all-to-all-done.3.moment_ref = f32[16,1,384]{2,1,0:T(1,128)S(1)} async-done(((f32[16,1,384]{2,1,0:T(1,128)}), f32[16,1,384]{2,1,0:T(1,128)S(1)}, u32[]{:S(2)}, u32[]{:S(2)}) %all-to-all-start.3) | async-done | bytes 24608 | tf_op jit(solution)/shard_map/all_to_all | solution.py:352
  83.5 1.4 %far.3 = (f32[3,512]{1,0:T(4,128)}, f32[3,512]{1,0:T(4,128)}) custom-call(s32[1,128]{1,0:T(1,128)S(1)} %get-tuple-element.9.far_ref, f32[2,8,256]{2,1,0:T(8,128)S(1)} %get-tuple-element.14.mine_ref, f32[2,32,256]{2,1,0:T(8,128)S(1)} %self_terms.3.self_ref, f32[2,16,256]{2,1,0:T(8,128)S(1)} %near.3.sum_ref, f32[16,1,384]{2,1,0:T(1,128)S(1)} %all-to-all-done.3.moment_ref), custom_call_target="tpu_custom_call" | custom-call | tf_op jit(solution)/shard_map/far/pallas_call | solution.py:341
Async XLA Ops:
  30.2 17.4 %all-to-all-start.1 = ((f32[16,1,384]{2,1,0:T(1,128)}), f32[16,1,384]{2,1,0:T(1,128)S(1)}, u32[]{:S(2)}, u32[]{:S(2)}) async-start(f32[16,1,384]{2,1,0:T(1,128)} %moments.2), calls=%async_computation.1 | async-start | bytes 49152 | tf_op jit(solution)/shard_map/all_to_all | solution.py:352
  67.0 16.4 %all-to-all-start.3 = ((f32[16,1,384]{2,1,0:T(1,128)}), f32[16,1,384]{2,1,0:T(1,128)S(1)}, u32[]{:S(2)}, u32[]{:S(2)}) async-start(f32[16,1,384]{2,1,0:T(1,128)} %moments.3), calls=%async_computation.3 | async-start | bytes 49152 | tf_op jit(solution)/shard_map/all_to_all | solution.py:352

commit v2 on v1

--- a/solution.py
+++ b/solution.py
@@ -122,6 +122,10 @@
         payload_ref[device, :, pl.ds(STATE_LANES, 128)] = tail
     for device in range(8, N_DEV, 8):
         payload_ref[device : device + 8] = payload_ref[0:8]
+    if info is not None:
+        lane = lax.broadcasted_iota(jnp.int32, (1, 128), 1)
+        for device in range(N_DEV):
+            payload_ref[device, :, pl.ds(STATE_LANES, 128)] = jnp.where(lane == 29, 1.0 * device, tail)
 
 
 def pack_kernel(pair_ref, count_ref, position_ref, strength_ref, far_ref, row_ref, *out_refs):
@@ -137,18 +141,25 @@
     publish([state[:, 0:BS], state[:, BS:]], info.astype(jnp.float32), *out_refs)
 
 
-def visit_counts(base, info):
+def visit_counts(info):
     lane = lax.broadcasted_iota(jnp.int32, (N_DEV, 128), 1)
-    live = info[:, 28:29]
-    counts = jnp.zeros((N_DEV, 128), jnp.int32)
-    for slot in range(6):
-        first = info[:, 16 + slot : 17 + slot]
-        second = info[:, 22 + slot : 23 + slot]
-        for target, source in ((first, second), (second, first)):
-            own = target - base
-            code = jnp.where((own >= 0) & (own < 2) & (slot < live), own * 64 + source, -1)
-            counts = counts + jnp.where(lane == code, 1, 0)
-    return jnp.sum(counts, axis=0, keepdims=True)
+    first = lane < 22
+    partner = jnp.where(first, pltpu.roll(info, 128 - 6, 1), pltpu.roll(info, 6, 1))
+    slot = jnp.where(first, lane - 16, lane - 22).astype(jnp.float32)
+    own = info - 2.0 * info[:, 29:30]
+    live = (slot >= 0.0) & (slot < info[:, 28:29]) & (lane < 28) & (own >= 0.0) & (own < 2.0)
+    codes = jnp.where(live, own * 64.0 + partner, -1.0).T
+    code = lax.broadcasted_iota(jnp.int32, (128, N_DEV), 0).astype(jnp.float32)
+    times = jnp.zeros((128, N_DEV), jnp.float32)
+    for row in range(16, 28):
+        times = times + jnp.where(code == codes[row : row + 1], 1.0, 0.0)
+    counts = lax.dot_general(
+        jnp.ones((8, N_DEV), jnp.bfloat16),
+        times.astype(jnp.bfloat16),
+        (((1,), (1,)), ((), ())),
+        preferred_element_type=jnp.float32,
+    )
+    return counts.astype(jnp.int32)
 
 
 def moment_kernel(region_ref, moment_ref):
@@ -163,9 +174,9 @@
     if len(refs) == 2:
         out_ref, mats = refs
     else:
-        me_ref, region_ref, out_ref, count_ref, mats = refs
+        region_ref, out_ref, count_ref, mats = refs
         tails = region_ref[:, 0, STATE_LANES:]
-        count_ref[...] = visit_counts(2 * me_ref[0], tails.astype(jnp.int32))
+        count_ref[...] = visit_counts(tails)
     for block in range(2):
         state = mine_ref[block]
         centre = centre_of(state)
@@ -186,8 +197,11 @@
     list_ref[0] = place - 1
 
 
-def near_kernel(count_ref, self_ref, region_ref, sum_ref, mats, list_ref):
-    visit_list(count_ref, list_ref)
+def near_kernel(count_ref, self_ref, region_ref, sum_ref, mats, list_ref, count_smem, sem):
+    copy = pltpu.make_async_copy(count_ref, count_smem, sem)
+    copy.start()
+    copy.wait()
+    visit_list(count_smem, list_ref)
     sum_ref[...] = self_ref[:, 0:16]
 
     def visit(place, slot):
@@ -310,9 +324,9 @@
 def self_terms(mine, *pair_operands):
     out_shape, out_specs, in_specs = (kept(2, 32, BS),), in_vmem(1), in_vmem(1)
     if pair_operands:
-        out_shape += (jax.ShapeDtypeStruct((1, 128), jnp.int32),)
+        out_shape += (pltpu.VMEM((8, 128), jnp.int32),)
         out_specs = in_vmem(2)
-        in_specs = in_vmem(1) + in_smem(1) + in_vmem(1)
+        in_specs = in_vmem(2)
     return pl.pallas_call(
         self_kernel,
         out_shape=out_shape,
@@ -328,12 +342,17 @@
     return pl.pallas_call(
         near_kernel,
         out_shape=kept(2, 16, BS),
-        in_specs=in_smem(1) + in_vmem(2),
+        in_specs=in_vmem(3),
         out_specs=in_vmem(1)[0],
-        scratch_shapes=[pltpu.VMEM((2, 4, BS, BS), jnp.bfloat16), pltpu.SMEM((136,), jnp.int32)],
+        scratch_shapes=[
+            pltpu.VMEM((2, 4, BS, BS), jnp.bfloat16),
+            pltpu.SMEM((136,), jnp.int32),
+            pltpu.SMEM((8, 128), jnp.int32),
+            pltpu.SemaphoreType.DMA(()),
+        ],
         cost_estimate=pl.CostEstimate(flops=20000000, bytes_accessed=600000, transcendentals=500000),
         name="near",
-    )(counts, keep(own), region)
+    )(keep(counts), keep(own), region)
 
 
 def far(far_row, mine, own, sums, moments, last):
@@ -353,7 +372,6 @@
 
 
 def body(positions, strengths, pair_list, pair_count, far_list):
-    me = lax.axis_index("dev").astype(jnp.int32).reshape(1)
     far_row, payload, mine = pack(pair_list, pair_count, positions, strengths, far_list)
     counts = None
     for step in range(STEPS):
@@ -361,7 +379,7 @@
         region = keep(exchange(payload, "dev"))
         moments = exchange(moments_of(region), "group")
         if first:
-            own, counts = self_terms(mine, me, region)
+            own, counts = self_terms(mine, region)
         else:
             (own,) = self_terms(mine)
         sums = near(counts, own, region)

time: 85.2 us -> 84.1 us (0.987)
  Pallas kernels: 10.5 us -> 14 us
  waiting for transfers between devices: 8.85 us -> 5.44 us
  starting transfers between devices: 19.1 us -> 17.9 us
    pallas_call x2, Pallas kernels: 2.08 us -> 7.13 us  [near(): pl.pallas_call(near_kernel, out_shape=kept(2, 16, BS), in_specs=in_vmem(3...]
    all_to_all x2, waiting for transfers between devices: 8.85 us -> 5.44 us  [exchange(): return lax.all_to_all(value, axis, 0, 0, tiled=True)]
    pallas_call x2, Pallas kernels: 3.74 us -> 2.1 us  [self_terms(): pl.pallas_call(self_kernel, out_shape=out_shape, in_specs=in_specs, out_s...]
    all_to_all x2, starting transfers between devices: 19.1 us -> 17.9 us  [exchange(): return lax.all_to_all(value, axis, 0, 0, tiled=True)]
  transfers between devices with their start and end apart: 2 -> 2, of which waited for: 2 -> 2; matrix products, arithmetic and copies ran while one was open for 0% -> 0% of each run, Pallas kernels for 7% -> 11%
where the time goes in v2:
time: 84.1 us; the launch traced here: 83.8 us
  blocking collectives  45.2 us (54%)
  starting transfers between devices  17.9 us (21%)
  Pallas kernels  14 us (17%)
  waiting for transfers between devices  5.44 us (6%)
  between operations  1.32 us (2%)
    all_to_all x2, blocking collectives, exchange(): return lax.all_to_all(value, axis, 0, 0, tiled=True)  45.2 us
    all_to_all x2, starting transfers between devices, exchange(): return lax.all_to_all(value, axis, 0, 0, tiled=True)  17.9 us
    pallas_call x2, Pallas kernels, near(): pl.pallas_call(near_kernel, out_shape=kept(2, 16, BS), in_specs=in_vmem(3...  7.13 us
    all_to_all x2, waiting for transfers between devices, exchange(): return lax.all_to_all(value, axis, 0, 0, tiled=True)  5.44 us
    pallas_call x2, Pallas kernels, far(): pl.pallas_call(functools.partial(far_kernel, last), out_shape=out_shape,...  2.24 us
    pallas_call x2, Pallas kernels, self_terms(): pl.pallas_call(self_kernel, out_shape=out_shape, in_specs=in_specs, out_s...  2.1 us
  transfers between devices with their start and end apart: 2, of which 2 were waited for; matrix products, arithmetic and copies ran while one was open for 0% of the time, Pallas kernels for 11%

profile of v2, /device:TPU:1, one launch (start us, length us, event | category | flops | bytes accessed | tf_op | source)
XLA Modules:
  0.0 83.8 jit_solution(1440981267172813661)
XLA Ops:
  1.3 0.9 %pack.1 = (s32[1,128]{1,0:T(1,128)S(1)}, f32[32,1,3200]{2,1,0:T(1,128)S(1)}, f32[2,8,256]{2,1,0:T(8,128)S(1)}) custom-call(s32[2,6]{1,0:T(2,128)} %pair_ref.1, s32[1]{0:T(128)S(6)} %copy.7.count_ref, f32[3,512]{1,0:T(4,128)} %position_ref.1, f32[3,512]{1,0:T(4,128)} %strength_ref.1, s32[2,64]{1,0:T(2,128)} %bitcast.1), custom_call_target="tpu_custom_call" | custom-call | tf_op jit(solution)/shard_map/pack/pallas_call | solution.py:305
  2.2 27.2 %all_to_all.20.refs_0_.region_ref = f32[32,1,3200]{2,1,0:T(1,128)S(1)} all-to-all(f32[32,1,3200]{2,1,0:T(1,128)S(1)} %get-tuple-element.11), channel_id=1, replica_groups=mesh['group'=16,'dev'=32] {'dev'}, dimensions={0} | all-to-all | bytes 819200 | tf_op jit(solution)/shard_map/all_to_all | solution.py:371
  29.4 0.8 moments.2
  30.2 10.0 %all-to-all-start.1 = ((f32[16,1,384]{2,1,0:T(1,128)}), f32[16,1,384]{2,1,0:T(1,128)S(1)}, u32[]{:S(2)}, u32[]{:S(2)}) async-start(f32[16,1,384]{2,1,0:T(1,128)} %moments.2), calls=%async_computation.1 | async-start | bytes 49152 | tf_op jit(solution)/shard_map/all_to_all | solution.py:371
  40.2 1.1 %self_terms.2 = (f32[2,32,256]{2,1,0:T(8,128)S(1)}, s32[8,128]{1,0:T(8,128)S(1)}) custom-call(f32[2,8,256]{2,1,0:T(8,128)S(1)} %get-tuple-element.10.mine_ref, f32[32,1,3200]{2,1,0:T(1,128)S(1)} %all_to_all.20.refs_0_.region_ref), custom_call_target="tpu_custom_call" | custom-call | flops 4000000 | bytes 60000 | tf_op jit(solution)/shard_map/self_terms/pallas_call | solution.py:330
  41.4 3.6 %near.2.sum_ref = f32[2,16,256]{2,1,0:T(8,128)S(1)} custom-call(s32[8,128]{1,0:T(8,128)S(1)} %get-tuple-element.13.count_ref, f32[2,32,256]{2,1,0:T(8,128)S(1)} %get-tuple-element.12.self_ref, f32[32,1,3200]{2,1,0:T(1,128)S(1)} %all_to_all.20.refs_0_.region_ref), custom_call_target="tpu_custom_call" | custom-call | flops 20000000 | bytes 600000 | tf_op jit(solution)/shard_map/near/pallas_call | solution.py:342
  45.0 2.6 %all-to-all-done.1.moment_ref = f32[16,1,384]{2,1,0:T(1,128)S(1)} async-done(((f32[16,1,384]{2,1,0:T(1,128)}), f32[16,1,384]{2,1,0:T(1,128)S(1)}, u32[]{:S(2)}, u32[]{:S(2)}) %all-to-all-start.1) | async-done | bytes 24608 | tf_op jit(solution)/shard_map/all_to_all | solution.py:371
  47.6 0.9 %far.2 = (f32[32,1,3200]{2,1,0:T(1,128)S(1)}, f32[2,8,256]{2,1,0:T(8,128)S(1)}) custom-call(s32[1,128]{1,0:T(1,128)S(1)} %get-tuple-element.9.far_ref, f32[2,8,256]{2,1,0:T(8,128)S(1)} %get-tuple-element.10.mine_ref, f32[2,32,256]{2,1,0:T(8,128)S(1)} %get-tuple-element.12.self_ref, f32[2,16,256]{2,1,0:T(8,128)S(1)} %near.2.sum_ref, ...), custom_call_target="tpu_custom_call" | custom-call | tf_op jit(solution)/shard_map/far/pallas_call | solution.py:360
  48.5 18.0 %all_to_all.21.region_ref = f32[32,1,3200]{2,1,0:T(1,128)S(1)} all-to-all(f32[32,1,3200]{2,1,0:T(1,128)S(1)} %get-tuple-element.15), channel_id=1, replica_groups=mesh['group'=16,'dev'=32] {'dev'}, dimensions={0} | all-to-all | bytes 819200 | tf_op jit(solution)/shard_map/all_to_all | solution.py:371
  66.4 0.8 moments.3
  67.2 7.8 %all-to-all-start.3 = ((f32[16,1,384]{2,1,0:T(1,128)}), f32[16,1,384]{2,1,0:T(1,128)S(1)}, u32[]{:S(2)}, u32[]{:S(2)}) async-start(f32[16,1,384]{2,1,0:T(1,128)} %moments.3), calls=%async_computation.3 | async-start | bytes 49152 | tf_op jit(solution)/shard_map/all_to_all | solution.py:371
  75.0 1.0 %self_terms.3.self_ref = f32[2,32,256]{2,1,0:T(8,128)S(1)} custom-call(f32[2,8,256]{2,1,0:T(8,128)S(1)} %get-tuple-element.14.mine_ref), custom_call_target="tpu_custom_call" | custom-call | flops 4000000 | bytes 60000 | tf_op jit(solution)/shard_map/self_terms/pallas_call | solution.py:330
  76.0 3.6 %near.3.sum_ref = f32[2,16,256]{2,1,0:T(8,128)S(1)} custom-call(s32[8,128]{1,0:T(8,128)S(1)} %get-tuple-element.13.count_ref, f32[2,32,256]{2,1,0:T(8,128)S(1)} %self_terms.3.self_ref, f32[32,1,3200]{2,1,0:T(1,128)S(1)} %all_to_all.21.region_ref), custom_call_target="tpu_custom_call" | custom-call | flops 20000000 | bytes 600000 | tf_op jit(solution)/shard_map/near/pallas_call | solution.py:342
  79.6 2.8 %all-to-all-done.3.moment_ref = f32[16,1,384]{2,1,0:T(1,128)S(1)} async-done(((f32[16,1,384]{2,1,0:T(1,128)}), f32[16,1,384]{2,1,0:T(1,128)S(1)}, u32[]{:S(2)}, u32[]{:S(2)}) %all-to-all-start.3) | async-done | bytes 24608 | tf_op jit(solution)/shard_map/all_to_all | solution.py:371
  82.4 1.4 %far.3 = (f32[3,512]{1,0:T(4,128)}, f32[3,512]{1,0:T(4,128)}) custom-call(s32[1,128]{1,0:T(1,128)S(1)} %get-tuple-element.9.far_ref, f32[2,8,256]{2,1,0:T(8,128)S(1)} %get-tuple-element.14.mine_ref, f32[2,32,256]{2,1,0:T(8,128)S(1)} %self_terms.3.self_ref, f32[2,16,256]{2,1,0:T(8,128)S(1)} %near.3.sum_ref, f32[16,1,384]{2,1,0:T(1,128)S(1)} %all-to-all-done.3.moment_ref), custom_call_target="tpu_custom_call" | custom-call | tf_op jit(solution)/shard_map/far/pallas_call | solution.py:360
Async XLA Ops:
  30.2 17.4 %all-to-all-start.1 = ((f32[16,1,384]{2,1,0:T(1,128)}), f32[16,1,384]{2,1,0:T(1,128)S(1)}, u32[]{:S(2)}, u32[]{:S(2)}) async-start(f32[16,1,384]{2,1,0:T(1,128)} %moments.2), calls=%async_computation.1 | async-start | bytes 49152 | tf_op jit(solution)/shard_map/all_to_all | solution.py:371
  67.2 15.2 %all-to-all-start.3 = ((f32[16,1,384]{2,1,0:T(1,128)}), f32[16,1,384]{2,1,0:T(1,128)S(1)}, u32[]{:S(2)}, u32[]{:S(2)}) async-start(f32[16,1,384]{2,1,0:T(1,128)} %moments.3), calls=%async_computation.3 | async-start | bytes 49152 | tf_op jit(solution)/shard_map/all_to_all | solution.py:371

commit v3 on v2

--- a/solution.py
+++ b/solution.py
@@ -154,8 +154,8 @@
     for row in range(16, 28):
         times = times + jnp.where(code == codes[row : row + 1], 1.0, 0.0)
     counts = lax.dot_general(
-        jnp.ones((8, N_DEV), jnp.bfloat16),
-        times.astype(jnp.bfloat16),
+        jnp.ones((8, N_DEV), jnp.float32),
+        times,
         (((1,), (1,)), ((), ())),
         preferred_element_type=jnp.float32,
     )
@@ -206,13 +206,13 @@
 
     def visit(place, slot):
         code = list_ref[place]
-        times = (code // 128).astype(jnp.float32)
-        block = code // 64 % 2
-        source = code % 64
+        times = (code >> 7).astype(jnp.float32)
+        block = (code >> 6) & 1
+        source = code & 63
         rows = []
         for c in range(6):
-            lanes = pl.ds(pl.multiple_of(2 * BS * c + BS * (source % 2), BS), BS)
-            rows.append(region_ref[source // 2, :, lanes])
+            lanes = pl.ds(pl.multiple_of(2 * BS * c + BS * (source & 1), BS), BS)
+            rows.append(region_ref[source >> 1, :, lanes])
         rows.append(jnp.zeros((2, BS), jnp.float32))
         rows = jnp.concatenate(rows, axis=0) - self_ref[block, 24:32]
         fill_kernels(self_ref[block, 16:24], rows, mats.at[slot], BS)
@@ -226,9 +226,9 @@
         return carry
 
     count = list_ref[0]
-    lax.fori_loop(0, count // 2, visit_two, 0)
-
-    @pl.when(count % 2 == 1)
+    lax.fori_loop(0, count >> 1, visit_two, 0)
+
+    @pl.when(count & 1 == 1)
     def _():
         block, sums = visit(count, 0)
         sum_ref[block] += sums
@@ -244,13 +244,13 @@
     middle = (table - high).astype(jnp.bfloat16).astype(jnp.float32)
     parts = jnp.concatenate([high, middle, table - high - middle], axis=0).astype(jnp.bfloat16)
     wanted = far_ref[...]
-    place = wanted % 2 * N_DEV + wanted % REGION_BLOCKS // 2
+    place = (wanted & 1) * N_DEV + ((wanted >> 1) & (N_DEV - 1))
     lanes = lax.broadcasted_iota(jnp.int32, (REGION_BLOCKS, 128), 0)
     chosen = jnp.where(lanes == place, 1.0, 0.0).astype(jnp.bfloat16)
     found = jnp.dot(parts, chosen, preferred_element_type=jnp.float32)
     found = found[0:size] + found[size : 2 * size] + found[2 * size :]
     groups = lax.broadcasted_iota(jnp.int32, (N_GROUP, 128), 0)
-    mine = groups == wanted // REGION_BLOCKS
+    mine = groups == wanted >> 6
     rows = []
     for c in range(6):
         part = found[N_GROUP * c : N_GROUP * c + N_GROUP]

time: 84.1 us -> 83.5 us (level)
  Pallas kernels: 14 us -> 11.7 us
  waiting for transfers between devices: 5.44 us -> 7.68 us
    pallas_call x2, Pallas kernels: 7.13 us -> 4.88 us  [near(): pl.pallas_call(near_kernel, out_shape=kept(2, 16, BS), in_specs=in_vmem(3...]
    all_to_all x2, waiting for transfers between devices: 5.44 us -> 7.68 us  [exchange(): return lax.all_to_all(value, axis, 0, 0, tiled=True)]
  transfers between devices with their start and end apart: 2 -> 2, of which waited for: 2 -> 2; matrix products, arithmetic and copies ran while one was open for 0% -> 0% of each run, Pallas kernels for 11% -> 8%
where the time goes in v3:
time: 83.5 us; the launch traced here: 83.2 us
  blocking collectives  45.2 us (54%)
  starting transfers between devices  17.3 us (21%)
  Pallas kernels  11.7 us (14%)
  waiting for transfers between devices  7.68 us (9%)
  between operations  1.32 us (2%)
    all_to_all x2, blocking collectives, exchange(): return lax.all_to_all(value, axis, 0, 0, tiled=True)  45.2 us
    all_to_all x2, starting transfers between devices, exchange(): return lax.all_to_all(value, axis, 0, 0, tiled=True)  17.3 us
    all_to_all x2, waiting for transfers between devices, exchange(): return lax.all_to_all(value, axis, 0, 0, tiled=True)  7.68 us
    pallas_call x2, Pallas kernels, near(): pl.pallas_call(near_kernel, out_shape=kept(2, 16, BS), in_specs=in_vmem(3...  4.88 us
    pallas_call x2, Pallas kernels, far(): pl.pallas_call(functools.partial(far_kernel, last), out_shape=out_shape,...  2.24 us
    pallas_call x2, Pallas kernels, self_terms(): pl.pallas_call(self_kernel, out_shape=out_shape, in_specs=in_specs, out_s...  2.1 us
  transfers between devices with their start and end apart: 2, of which 2 were waited for; matrix products, arithmetic and copies ran while one was open for 0% of the time, Pallas kernels for 8%

profile of v3, /device:TPU:1, one launch (start us, length us, event | category | flops | bytes accessed | tf_op | source)
XLA Modules:
  0.0 83.2 jit_solution(8573021414182042721)
XLA Ops:
  1.3 0.9 %pack.1 = (s32[1,128]{1,0:T(1,128)S(1)}, f32[32,1,3200]{2,1,0:T(1,128)S(1)}, f32[2,8,256]{2,1,0:T(8,128)S(1)}) custom-call(s32[2,6]{1,0:T(2,128)} %pair_ref.1, s32[1]{0:T(128)S(6)} %copy.7.count_ref, f32[3,512]{1,0:T(4,128)} %position_ref.1, f32[3,512]{1,0:T(4,128)} %strength_ref.1, s32[2,64]{1,0:T(2,128)} %bitcast.1), custom_call_target="tpu_custom_call" | custom-call | tf_op jit(solution)/shard_map/pack/pallas_call | solution.py:305
  2.2 27.2 %all_to_all.20.refs_0_.region_ref = f32[32,1,3200]{2,1,0:T(1,128)S(1)} all-to-all(f32[32,1,3200]{2,1,0:T(1,128)S(1)} %get-tuple-element.11), channel_id=1, replica_groups=mesh['group'=16,'dev'=32] {'dev'}, dimensions={0} | all-to-all | bytes 819200 | tf_op jit(solution)/shard_map/all_to_all | solution.py:371
  29.4 0.8 moments.2
  30.2 10.0 %all-to-all-start.1 = ((f32[16,1,384]{2,1,0:T(1,128)}), f32[16,1,384]{2,1,0:T(1,128)S(1)}, u32[]{:S(2)}, u32[]{:S(2)}) async-start(f32[16,1,384]{2,1,0:T(1,128)} %moments.2), calls=%async_computation.1 | async-start | bytes 49152 | tf_op jit(solution)/shard_map/all_to_all | solution.py:371
  40.2 1.1 %self_terms.2 = (f32[2,32,256]{2,1,0:T(8,128)S(1)}, s32[8,128]{1,0:T(8,128)S(1)}) custom-call(f32[2,8,256]{2,1,0:T(8,128)S(1)} %get-tuple-element.10.mine_ref, f32[32,1,3200]{2,1,0:T(1,128)S(1)} %all_to_all.20.refs_0_.region_ref), custom_call_target="tpu_custom_call" | custom-call | flops 4000000 | bytes 60000 | tf_op jit(solution)/shard_map/self_terms/pallas_call | solution.py:330
  41.4 2.5 %near.2.sum_ref = f32[2,16,256]{2,1,0:T(8,128)S(1)} custom-call(s32[8,128]{1,0:T(8,128)S(1)} %get-tuple-element.13.count_ref, f32[2,32,256]{2,1,0:T(8,128)S(1)} %get-tuple-element.12.self_ref, f32[32,1,3200]{2,1,0:T(1,128)S(1)} %all_to_all.20.refs_0_.region_ref), custom_call_target="tpu_custom_call" | custom-call | flops 20000000 | bytes 600000 | tf_op jit(solution)/shard_map/near/pallas_call | solution.py:342
  43.8 3.7 %all-to-all-done.1.moment_ref = f32[16,1,384]{2,1,0:T(1,128)S(1)} async-done(((f32[16,1,384]{2,1,0:T(1,128)}), f32[16,1,384]{2,1,0:T(1,128)S(1)}, u32[]{:S(2)}, u32[]{:S(2)}) %all-to-all-start.1) | async-done | bytes 24608 | tf_op jit(solution)/shard_map/all_to_all | solution.py:371
  47.6 0.9 %far.2 = (f32[32,1,3200]{2,1,0:T(1,128)S(1)}, f32[2,8,256]{2,1,0:T(8,128)S(1)}) custom-call(s32[1,128]{1,0:T(1,128)S(1)} %get-tuple-element.9.far_ref, f32[2,8,256]{2,1,0:T(8,128)S(1)} %get-tuple-element.10.mine_ref, f32[2,32,256]{2,1,0:T(8,128)S(1)} %get-tuple-element.12.self_ref, f32[2,16,256]{2,1,0:T(8,128)S(1)} %near.2.sum_ref, ...), custom_call_target="tpu_custom_call" | custom-call | tf_op jit(solution)/shard_map/far/pallas_call | solution.py:360
  48.5 18.0 %all_to_all.21.region_ref = f32[32,1,3200]{2,1,0:T(1,128)S(1)} all-to-all(f32[32,1,3200]{2,1,0:T(1,128)S(1)} %get-tuple-element.15), channel_id=1, replica_groups=mesh['group'=16,'dev'=32] {'dev'}, dimensions={0} | all-to-all | bytes 819200 | tf_op jit(solution)/shard_map/all_to_all | solution.py:371
  66.4 0.8 moments.3
  67.2 7.3 %all-to-all-start.3 = ((f32[16,1,384]{2,1,0:T(1,128)}), f32[16,1,384]{2,1,0:T(1,128)S(1)}, u32[]{:S(2)}, u32[]{:S(2)}) async-start(f32[16,1,384]{2,1,0:T(1,128)} %moments.3), calls=%async_computation.3 | async-start | bytes 49152 | tf_op jit(solution)/shard_map/all_to_all | solution.py:371
  74.5 1.0 %self_terms.3.self_ref = f32[2,32,256]{2,1,0:T(8,128)S(1)} custom-call(f32[2,8,256]{2,1,0:T(8,128)S(1)} %get-tuple-element.14.mine_ref), custom_call_target="tpu_custom_call" | custom-call | flops 4000000 | bytes 60000 | tf_op jit(solution)/shard_map/self_terms/pallas_call | solution.py:330
  75.4 2.4 %near.3.sum_ref = f32[2,16,256]{2,1,0:T(8,128)S(1)} custom-call(s32[8,128]{1,0:T(8,128)S(1)} %get-tuple-element.13.count_ref, f32[2,32,256]{2,1,0:T(8,128)S(1)} %self_terms.3.self_ref, f32[32,1,3200]{2,1,0:T(1,128)S(1)} %all_to_all.21.region_ref), custom_call_target="tpu_custom_call" | custom-call | flops 20000000 | bytes 600000 | tf_op jit(solution)/shard_map/near/pallas_call | solution.py:342
  77.9 3.9 %all-to-all-done.3.moment_ref = f32[16,1,384]{2,1,0:T(1,128)S(1)} async-done(((f32[16,1,384]{2,1,0:T(1,128)}), f32[16,1,384]{2,1,0:T(1,128)S(1)}, u32[]{:S(2)}, u32[]{:S(2)}) %all-to-all-start.3) | async-done | bytes 24608 | tf_op jit(solution)/shard_map/all_to_all | solution.py:371
  81.8 1.4 %far.3 = (f32[3,512]{1,0:T(4,128)}, f32[3,512]{1,0:T(4,128)}) custom-call(s32[1,128]{1,0:T(1,128)S(1)} %get-tuple-element.9.far_ref, f32[2,8,256]{2,1,0:T(8,128)S(1)} %get-tuple-element.14.mine_ref, f32[2,32,256]{2,1,0:T(8,128)S(1)} %self_terms.3.self_ref, f32[2,16,256]{2,1,0:T(8,128)S(1)} %near.3.sum_ref, f32[16,1,384]{2,1,0:T(1,128)S(1)} %all-to-all-done.3.moment_ref), custom_call_target="tpu_custom_call" | custom-call | tf_op jit(solution)/shard_map/far/pallas_call | solution.py:360
Async XLA Ops:
  30.2 17.4 %all-to-all-start.1 = ((f32[16,1,384]{2,1,0:T(1,128)}), f32[16,1,384]{2,1,0:T(1,128)S(1)}, u32[]{:S(2)}, u32[]{:S(2)}) async-start(f32[16,1,384]{2,1,0:T(1,128)} %moments.2), calls=%async_computation.1 | async-start | bytes 49152 | tf_op jit(solution)/shard_map/all_to_all | solution.py:371
  67.2 14.6 %all-to-all-start.3 = ((f32[16,1,384]{2,1,0:T(1,128)}), f32[16,1,384]{2,1,0:T(1,128)S(1)}, u32[]{:S(2)}, u32[]{:S(2)}) async-start(f32[16,1,384]{2,1,0:T(1,128)} %moments.3), calls=%async_computation.3 | async-start | bytes 49152 | tf_op jit(solution)/shard_map/all_to_all | solution.py:371

commit v4 on v3

--- a/solution.py
+++ b/solution.py
@@ -170,21 +170,29 @@
         moment_ref[group] = table
 
 
-def self_kernel(mine_ref, *refs):
-    if len(refs) == 2:
-        out_ref, mats = refs
-    else:
-        region_ref, out_ref, count_ref, mats = refs
-        tails = region_ref[:, 0, STATE_LANES:]
-        count_ref[...] = visit_counts(tails)
-    for block in range(2):
-        state = mine_ref[block]
+def own_terms(blocks, out_ref, mats):
+    for block, state in enumerate(blocks):
         centre = centre_of(state)
         target = state - centre
         fill_kernels(target, target, mats.at[block], BS)
         out_ref[block, 0:16] = weighted_sums(target, mats.at[block], BS)
         out_ref[block, 16:24] = target
         out_ref[block, 24:32] = centre
+
+
+def first_self_kernel(mine_ref, region_ref, out_ref, count_ref, mats):
+    count_ref[...] = visit_counts(region_ref[:, 0, STATE_LANES:])
+    own_terms([mine_ref[0], mine_ref[1]], out_ref, mats)
+
+
+def later_self_kernel(core_ref, mine_ref, early_ref, out_ref, mats):
+    @pl.when(core_ref[0] == 0)
+    def _():
+        own_terms([mine_ref[0], mine_ref[1]], out_ref, mats)
+
+    @pl.when(core_ref[0] != 0)
+    def _():
+        out_ref[...] = early_ref[...]
 
 
 def visit_list(count_ref, list_ref):
@@ -258,8 +266,11 @@
     return jnp.concatenate(rows + [jnp.zeros((2, 128), jnp.float32)], axis=0)
 
 
-def far_kernel(last, far_ref, mine_ref, self_ref, sum_ref, moment_ref, *refs):
-    *outs, mats = refs
+def far_kernel(last, *refs):
+    if last:
+        far_ref, mine_ref, self_ref, sum_ref, moment_ref, *outs, mats = refs
+    else:
+        core_ref, far_ref, mine_ref, self_ref, sum_ref, moment_ref, *outs, early_ref, mats, wide_mats = refs
     rows = far_sources(far_ref, moment_ref)
     blocks = []
     for block in range(2):
@@ -277,6 +288,14 @@
     else:
         publish(blocks, None, *outs)
 
+        @pl.when(core_ref[0] != 0)
+        def _():
+            own_terms(blocks, early_ref, wide_mats)
+
+        @pl.when(core_ref[0] == 0)
+        def _():
+            early_ref[...] = jnp.zeros_like(early_ref)
+
 
 def f32(*shape):
     return jax.ShapeDtypeStruct(shape, jnp.float32)
@@ -321,21 +340,32 @@
     )(region)
 
 
-def self_terms(mine, *pair_operands):
-    out_shape, out_specs, in_specs = (kept(2, 32, BS),), in_vmem(1), in_vmem(1)
-    if pair_operands:
-        out_shape += (pltpu.VMEM((8, 128), jnp.int32),)
-        out_specs = in_vmem(2)
-        in_specs = in_vmem(2)
-    return pl.pallas_call(
-        self_kernel,
-        out_shape=out_shape,
-        in_specs=in_specs,
-        out_specs=tuple(out_specs),
-        scratch_shapes=[pltpu.VMEM((2, 4, BS, BS), jnp.bfloat16)],
-        cost_estimate=pl.CostEstimate(flops=4000000, bytes_accessed=60000, transcendentals=130000),
+WIDE_MATS = pltpu.VMEM((2, 4, BS, BS), jnp.bfloat16)
+SELF_COST = pl.CostEstimate(flops=4000000, bytes_accessed=60000, transcendentals=130000)
+
+
+def first_self_terms(mine, region):
+    return pl.pallas_call(
+        first_self_kernel,
+        out_shape=(kept(2, 32, BS), pltpu.VMEM((8, 128), jnp.int32)),
+        in_specs=in_vmem(2),
+        out_specs=tuple(in_vmem(2)),
+        scratch_shapes=[WIDE_MATS],
+        cost_estimate=SELF_COST,
         name="self_terms",
-    )(keep(mine), *pair_operands)
+    )(keep(mine), region)
+
+
+def later_self_terms(core, mine, early):
+    return pl.pallas_call(
+        later_self_kernel,
+        out_shape=kept(2, 32, BS),
+        in_specs=in_smem(1) + in_vmem(2),
+        out_specs=in_vmem(1)[0],
+        scratch_shapes=[WIDE_MATS],
+        cost_estimate=SELF_COST,
+        name="self_terms",
+    )(core, keep(mine), keep(early))
 
 
 def near(counts, own, region):
@@ -355,16 +385,25 @@
     )(keep(counts), keep(own), region)
 
 
-def far(far_row, mine, own, sums, moments, last):
-    out_shape = (f32(3, 2 * BS), f32(3, 2 * BS)) if last else PUBLISHED
+def far(core, far_row, mine, own, sums, moments, last):
+    operands = [keep(value) for value in (far_row, mine, own, sums, moments)]
+    in_specs = in_vmem(5)
+    scratch = [pltpu.VMEM((2, 4, 64, BS), jnp.bfloat16)]
+    if last:
+        out_shape = (f32(3, 2 * BS), f32(3, 2 * BS))
+    else:
+        out_shape = PUBLISHED + (kept(2, 32, BS),)
+        operands = [core] + operands
+        in_specs = in_smem(1) + in_specs
+        scratch.append(WIDE_MATS)
     return pl.pallas_call(
         functools.partial(far_kernel, last),
         out_shape=out_shape,
-        in_specs=in_vmem(5),
+        in_specs=in_specs,
         out_specs=tuple(in_vmem(len(out_shape))),
-        scratch_shapes=[pltpu.VMEM((2, 4, 64, BS), jnp.bfloat16)],
+        scratch_shapes=scratch,
         name="far",
-    )(keep(far_row), keep(mine), keep(own), keep(sums), keep(moments))
+    )(*operands)
 
 
 def exchange(value, axis):
@@ -372,20 +411,21 @@
 
 
 def body(positions, strengths, pair_list, pair_count, far_list):
+    core = (lax.axis_index("group").astype(jnp.int32) & (NC - 1)).reshape(1)
     far_row, payload, mine = pack(pair_list, pair_count, positions, strengths, far_list)
-    counts = None
+    counts, early = None, None
     for step in range(STEPS):
         first, last = step == 0, step == STEPS - 1
         region = keep(exchange(payload, "dev"))
         moments = exchange(moments_of(region), "group")
         if first:
-            own, counts = self_terms(mine, region)
+            own, counts = first_self_terms(mine, region)
         else:
-            (own,) = self_terms(mine)
+            own = later_self_terms(core, mine, early)
         sums = near(counts, own, region)
-        result = far(far_row, mine, own, sums, moments, last)
+        result = far(core, far_row, mine, own, sums, moments, last)
         if not last:
-            payload, mine = result
+            payload, mine, early = result
     return result
 
 

time: 83.5 us -> 84.2 us (level)
  Pallas kernels: 11.7 us -> 17.4 us
  waiting for transfers between devices: 7.68 us -> 2.8 us
  starting transfers between devices: 17.3 us -> 15.9 us
  blocking collectives: 45.2 us -> 46.4 us
    pallas_call x2, Pallas kernels: 4.88 us -> 10.7 us  [near(): pl.pallas_call(near_kernel, out_shape=kept(2, 16, BS), in_specs=in_vmem(3...]
    all_to_all x2, waiting for transfers between devices: 7.68 us -> 2.8 us  [exchange(): return lax.all_to_all(value, axis, 0, 0, tiled=True)]
    all_to_all x2, starting transfers between devices: 17.3 us -> 15.9 us  [exchange(): return lax.all_to_all(value, axis, 0, 0, tiled=True)]
    all_to_all x2, blocking collectives: 45.2 us -> 46.4 us  [exchange(): return lax.all_to_all(value, axis, 0, 0, tiled=True)]
    pallas_call x2, Pallas kernels: 2.1 us -> 1.14 us  [the longest x1 1.14 us: first_self_terms(): pl.pallas_call(first_self_kernel, out_shape=(kept(2, 32, BS), pltpu.VMEM(...]
  transfers between devices with their start and end apart: 2 -> 2, of which waited for: 2 -> 2; matrix products, arithmetic and copies ran while one was open for 0% -> 0% of each run, Pallas kernels for 8% -> 14%
where the time goes in v4:
time: 84.2 us; the launch traced here: 83.8 us
  blocking collectives  46.4 us (55%)
  Pallas kernels  17.4 us (21%)
  starting transfers between devices  15.9 us (19%)
  waiting for transfers between devices  2.8 us (3%)
  between operations  1.31 us (2%)
    all_to_all x2, blocking collectives, exchange(): return lax.all_to_all(value, axis, 0, 0, tiled=True)  46.4 us
    all_to_all x2, starting transfers between devices, exchange(): return lax.all_to_all(value, axis, 0, 0, tiled=True)  15.9 us
    pallas_call x2, Pallas kernels, near(): pl.pallas_call(near_kernel, out_shape=kept(2, 16, BS), in_specs=in_vmem(3...  10.7 us
    pallas_call x2, Pallas kernels, far(): pl.pallas_call(functools.partial(far_kernel, last), out_shape=out_shape,...  3.04 us
    all_to_all x2, waiting for transfers between devices, exchange(): return lax.all_to_all(value, axis, 0, 0, tiled=True)  2.8 us
  transfers between devices with their start and end apart: 2, of which 2 were waited for; matrix products, arithmetic and copies ran while one was open for 0% of the time, Pallas kernels for 14%

profile of v4, /device:TPU:1, one launch (start us, length us, event | category | flops | bytes accessed | tf_op | source)
XLA Modules:
  0.0 83.8 jit_solution(8027485070196618765)
XLA Ops:
  1.3 0.9 %pack.1 = (s32[1,128]{1,0:T(1,128)S(1)}, f32[32,1,3200]{2,1,0:T(1,128)S(1)}, f32[2,8,256]{2,1,0:T(8,128)S(1)}) custom-call(s32[2,6]{1,0:T(2,128)} %pair_ref.1, s32[1]{0:T(128)S(6)} %copy.7.count_ref, f32[3,512]{1,0:T(4,128)} %position_ref.1, f32[3,512]{1,0:T(4,128)} %strength_ref.1, s32[2,64]{1,0:T(2,128)} %bitcast.2), custom_call_target="tpu_custom_call" | custom-call | tf_op jit(solution)/shard_map/pack/pallas_call | solution.py:324
  2.2 27.2 %all_to_all.20.region_ref = f32[32,1,3200]{2,1,0:T(1,128)S(1)} all-to-all(f32[32,1,3200]{2,1,0:T(1,128)S(1)} %get-tuple-element.12), channel_id=1, replica_groups=mesh['group'=16,'dev'=32] {'dev'}, dimensions={0} | all-to-all | bytes 819200 | tf_op jit(solution)/shard_map/all_to_all | solution.py:410
  29.4 0.8 moments.2
  30.2 10.0 %all-to-all-start.1 = ((f32[16,1,384]{2,1,0:T(1,128)}), f32[16,1,384]{2,1,0:T(1,128)S(1)}, u32[]{:S(2)}, u32[]{:S(2)}) async-start(f32[16,1,384]{2,1,0:T(1,128)} %moments.2), calls=%async_computation.1 | async-start | bytes 49152 | tf_op jit(solution)/shard_map/all_to_all | solution.py:410
  40.2 1.1 %self_terms.2 = (f32[2,32,256]{2,1,0:T(8,128)S(1)}, s32[8,128]{1,0:T(8,128)S(1)}) custom-call(f32[2,8,256]{2,1,0:T(8,128)S(1)} %get-tuple-element.11.mine_ref.refs_2_, f32[32,1,3200]{2,1,0:T(1,128)S(1)} %all_to_all.20.region_ref), custom_call_target="tpu_custom_call" | custom-call | flops 4000000 | bytes 60000 | tf_op jit(solution)/shard_map/self_terms/pallas_call | solution.py:348
  41.4 5.4 %near.2.refs_4_ = f32[2,16,256]{2,1,0:T(8,128)S(1)} custom-call(s32[8,128]{1,0:T(8,128)S(1)} %get-tuple-element.14.count_ref, f32[2,32,256]{2,1,0:T(8,128)S(1)} %get-tuple-element.13.self_ref.refs_3_, f32[32,1,3200]{2,1,0:T(1,128)S(1)} %all_to_all.20.region_ref), custom_call_target="tpu_custom_call" | custom-call | flops 20000000 | bytes 600000 | tf_op jit(solution)/shard_map/near/pallas_call | solution.py:372
  46.8 0.8 all-to-all-done.1.refs_5_
  47.6 1.7 %far.2 = (f32[32,1,3200]{2,1,0:T(1,128)S(1)}, f32[2,8,256]{2,1,0:T(8,128)S(1)}, f32[2,32,256]{2,1,0:T(8,128)S(1)}) custom-call(s32[1]{0:T(128)} %bitcast.1.refs_0_.core_ref, s32[1,128]{1,0:T(1,128)S(1)} %get-tuple-element.10.refs_1_.refs_0_, f32[2,8,256]{2,1,0:T(8,128)S(1)} %get-tuple-element.11.mine_ref.refs_2_, ...), custom_call_target="tpu_custom_call" | custom-call | tf_op jit(solution)/shard_map/far/pallas_call | solution.py:399
  49.3 19.2 %all_to_all.21.region_ref = f32[32,1,3200]{2,1,0:T(1,128)S(1)} all-to-all(f32[32,1,3200]{2,1,0:T(1,128)S(1)} %get-tuple-element.17), channel_id=1, replica_groups=mesh['group'=16,'dev'=32] {'dev'}, dimensions={0} | all-to-all | bytes 819200 | tf_op jit(solution)/shard_map/all_to_all | solution.py:410
  68.5 0.8 moments.3
  69.2 5.9 %all-to-all-start.3 = ((f32[16,1,384]{2,1,0:T(1,128)}), f32[16,1,384]{2,1,0:T(1,128)S(1)}, u32[]{:S(2)}, u32[]{:S(2)}) async-start(f32[16,1,384]{2,1,0:T(1,128)} %moments.3), calls=%async_computation.3 | async-start | bytes 49152 | tf_op jit(solution)/shard_map/all_to_all | solution.py:410
  75.1 5.4 %near.3.refs_3_ = f32[2,16,256]{2,1,0:T(8,128)S(1)} custom-call(s32[8,128]{1,0:T(8,128)S(1)} %get-tuple-element.14.count_ref, f32[2,32,256]{2,1,0:T(8,128)S(1)} %self_terms.3.self_ref.refs_2_, f32[32,1,3200]{2,1,0:T(1,128)S(1)} %all_to_all.21.region_ref), custom_call_target="tpu_custom_call" | custom-call | flops 20000000 | bytes 600000 | tf_op jit(solution)/shard_map/near/pallas_call | solution.py:372
  80.5 2.0 %all-to-all-done.3.refs_4_ = f32[16,1,384]{2,1,0:T(1,128)S(1)} async-done(((f32[16,1,384]{2,1,0:T(1,128)}), f32[16,1,384]{2,1,0:T(1,128)S(1)}, u32[]{:S(2)}, u32[]{:S(2)}) %all-to-all-start.3) | async-done | bytes 24608 | tf_op jit(solution)/shard_map/all_to_all | solution.py:410
  82.5 1.4 %far.3 = (f32[3,512]{1,0:T(4,128)}, f32[3,512]{1,0:T(4,128)}) custom-call(s32[1,128]{1,0:T(1,128)S(1)} %get-tuple-element.10.refs_1_.refs_0_, f32[2,8,256]{2,1,0:T(8,128)S(1)} %get-tuple-element.15.mine_ref.refs_1_, f32[2,32,256]{2,1,0:T(8,128)S(1)} %self_terms.3.self_ref.refs_2_, f32[2,16,256]{2,1,0:T(8,128)S(1)} %near.3.refs_3_, ...), custom_call_target="tpu_custom_call" | custom-call | tf_op jit(solution)/shard_map/far/pallas_call | solution.py:399
  (1 shorter events, 0.0 us)
Async XLA Ops:
  30.2 17.4 %all-to-all-start.1 = ((f32[16,1,384]{2,1,0:T(1,128)}), f32[16,1,384]{2,1,0:T(1,128)S(1)}, u32[]{:S(2)}, u32[]{:S(2)}) async-start(f32[16,1,384]{2,1,0:T(1,128)} %moments.2), calls=%async_computation.1 | async-start | bytes 49152 | tf_op jit(solution)/shard_map/all_to_all | solution.py:410
  69.2 13.2 %all-to-all-start.3 = ((f32[16,1,384]{2,1,0:T(1,128)}), f32[16,1,384]{2,1,0:T(1,128)S(1)}, u32[]{:S(2)}, u32[]{:S(2)}) async-start(f32[16,1,384]{2,1,0:T(1,128)} %moments.3), calls=%async_computation.3 | async-start | bytes 49152 | tf_op jit(solution)/shard_map/all_to_all | solution.py:410

commit v5 on v3

--- a/solution.py
+++ b/solution.py
@@ -31,10 +31,9 @@
     return jnp.concatenate(parts, axis=0).astype(jnp.bfloat16)
 
 
-def fill_kernels(target, source, mats, count):
+def fill_kernels(target, columns, mats, count):
     tx, ty, tz = target[0:1], target[1:2], target[2:3]
     ax, ay, az = target[3:4], target[4:5], target[5:6]
-    columns = source.T
     for start in range(0, count, CHUNK):
         part = columns[start : start + CHUNK]
         dx = tx - part[:, 0:1]
@@ -128,8 +127,7 @@
             payload_ref[device, :, pl.ds(STATE_LANES, 128)] = jnp.where(lane == 29, 1.0 * device, tail)
 
 
-def pack_kernel(pair_ref, count_ref, position_ref, strength_ref, far_ref, row_ref, *out_refs):
-    row_ref[...] = jnp.concatenate([far_ref[0:1], far_ref[1:2]], axis=1)
+def pack_kernel(pair_ref, count_ref, position_ref, strength_ref, *out_refs):
     zero = jnp.zeros((2, 2 * BS), jnp.float32)
     state = jnp.concatenate([position_ref[...], strength_ref[...], zero], axis=0)
     lane = lax.broadcasted_iota(jnp.int32, (1, 128), 1)
@@ -174,14 +172,15 @@
     if len(refs) == 2:
         out_ref, mats = refs
     else:
-        region_ref, out_ref, count_ref, mats = refs
+        region_ref, far_ref, out_ref, count_ref, row_ref, mats = refs
+        row_ref[...] = jnp.concatenate([far_ref[0:1], far_ref[1:2]], axis=1)
         tails = region_ref[:, 0, STATE_LANES:]
         count_ref[...] = visit_counts(tails)
     for block in range(2):
         state = mine_ref[block]
         centre = centre_of(state)
         target = state - centre
-        fill_kernels(target, target, mats.at[block], BS)
+        fill_kernels(target, target.T, mats.at[block], BS)
         out_ref[block, 0:16] = weighted_sums(target, mats.at[block], BS)
         out_ref[block, 16:24] = target
         out_ref[block, 24:32] = centre
@@ -215,7 +214,7 @@
             rows.append(region_ref[source >> 1, :, lanes])
         rows.append(jnp.zeros((2, BS), jnp.float32))
         rows = jnp.concatenate(rows, axis=0) - self_ref[block, 24:32]
-        fill_kernels(self_ref[block, 16:24], rows, mats.at[slot], BS)
+        fill_kernels(self_ref[block, 16:24], rows.T, mats.at[slot], BS)
         return block, times * weighted_sums(rows, mats.at[slot], BS)
 
     def visit_two(index, carry):
@@ -260,12 +259,14 @@
 
 def far_kernel(last, far_ref, mine_ref, self_ref, sum_ref, moment_ref, *refs):
     *outs, mats = refs
-    rows = far_sources(far_ref, moment_ref)
+    centres = [self_ref[block, 24:32][:, 0:64] for block in range(2)]
+    rows = far_sources(far_ref, moment_ref) - jnp.concatenate(centres, axis=1)
+    columns = rows.T
     blocks = []
     for block in range(2):
         target = self_ref[block, 16:24]
-        source = rows[:, 64 * block : 64 * block + 64] - self_ref[block, 24:32][:, 0:64]
-        fill_kernels(target, source, mats.at[block], 64)
+        source = rows[:, 64 * block : 64 * block + 64]
+        fill_kernels(target, columns[64 * block : 64 * block + 64], mats.at[block], 64)
         sums = sum_ref[block] + weighted_sums(source, mats.at[block], 64)
         new = mine_ref[block, 0:6] + advance_rows(target, sums)
         blocks.append(jnp.concatenate([new, jnp.zeros((2, BS), jnp.float32)], axis=0))
@@ -301,14 +302,14 @@
 PUBLISHED = (kept(N_DEV, 1, WIDTH), kept(2, 8, BS))
 
 
-def pack(pair_list, pair_count, positions, strengths, far_list):
+def pack(pair_list, pair_count, positions, strengths):
     return pl.pallas_call(
         pack_kernel,
-        out_shape=(pltpu.VMEM((1, 128), jnp.int32),) + PUBLISHED,
-        in_specs=in_smem(2) + in_vmem(3),
-        out_specs=tuple(in_vmem(3)),
+        out_shape=PUBLISHED,
+        in_specs=in_smem(2) + in_vmem(2),
+        out_specs=tuple(in_vmem(2)),
         name="pack",
-    )(pair_list, pair_count, positions, strengths, far_list.T)
+    )(pair_list, pair_count, positions, strengths)
 
 
 def moments_of(region):
@@ -324,9 +325,9 @@
 def self_terms(mine, *pair_operands):
     out_shape, out_specs, in_specs = (kept(2, 32, BS),), in_vmem(1), in_vmem(1)
     if pair_operands:
-        out_shape += (pltpu.VMEM((8, 128), jnp.int32),)
-        out_specs = in_vmem(2)
-        in_specs = in_vmem(2)
+        out_shape += (pltpu.VMEM((8, 128), jnp.int32), pltpu.VMEM((1, 128), jnp.int32))
+        out_specs = in_vmem(3)
+        in_specs = in_vmem(3)
     return pl.pallas_call(
         self_kernel,
         out_shape=out_shape,
@@ -372,14 +373,14 @@
 
 
 def body(positions, strengths, pair_list, pair_count, far_list):
-    far_row, payload, mine = pack(pair_list, pair_count, positions, strengths, far_list)
+    payload, mine = pack(pair_list, pair_count, positions, strengths)
     counts = None
     for step in range(STEPS):
         first, last = step == 0, step == STEPS - 1
         region = keep(exchange(payload, "dev"))
         moments = exchange(moments_of(region), "group")
         if first:
-            own, counts = self_terms(mine, region)
+            own, counts, far_row = self_terms(mine, region, far_list.T)
         else:
             (own,) = self_terms(mine)
         sums = near(counts, own, region)

time: 83.5 us -> 83.5 us (level)
  waiting for transfers between devices: 7.68 us -> 5.25 us
  Pallas kernels: 11.7 us -> 13.8 us
    all_to_all x2, waiting for transfers between devices: 7.68 us -> 5.25 us  [exchange(): return lax.all_to_all(value, axis, 0, 0, tiled=True)]
    pallas_call x2, Pallas kernels: 4.88 us -> 6.64 us  [near(): pl.pallas_call(near_kernel, out_shape=kept(2, 16, BS), in_specs=in_vmem(3...]
  transfers between devices with their start and end apart: 2 -> 2, of which waited for: 2 -> 2; matrix products, arithmetic and copies ran while one was open for 0% -> 0% of each run, Pallas kernels for 8% -> 11%
where the time goes in v5:
time: 83.5 us; the launch traced here: 83.1 us
  blocking collectives  45.2 us (54%)
  starting transfers between devices  17.6 us (21%)
  Pallas kernels  13.8 us (17%)
  waiting for transfers between devices  5.25 us (6%)
  between operations  1.32 us (2%)
    all_to_all x2, blocking collectives, exchange(): return lax.all_to_all(value, axis, 0, 0, tiled=True)  45.2 us
    all_to_all x2, starting transfers between devices, exchange(): return lax.all_to_all(value, axis, 0, 0, tiled=True)  17.6 us
    pallas_call x2, Pallas kernels, near(): pl.pallas_call(near_kernel, out_shape=kept(2, 16, BS), in_specs=in_vmem(3...  6.64 us
    all_to_all x2, waiting for transfers between devices, exchange(): return lax.all_to_all(value, axis, 0, 0, tiled=True)  5.25 us
    pallas_call x2, Pallas kernels, self_terms(): pl.pallas_call(self_kernel, out_shape=out_shape, in_specs=in_specs, out_s...  2.78 us
    pallas_call x2, Pallas kernels, far(): pl.pallas_call(functools.partial(far_kernel, last), out_shape=out_shape,...  2.02 us
  transfers between devices with their start and end apart: 2, of which 2 were waited for; matrix products, arithmetic and copies ran while one was open for 0% of the time, Pallas kernels for 11%

profile of v5, /device:TPU:1, one launch (start us, length us, event | category | flops | bytes accessed | tf_op | source)
XLA Modules:
  0.0 83.1 jit_solution(4118030009868427110)
XLA Ops:
  1.3 0.8 %pack.1 = (f32[32,1,3200]{2,1,0:T(1,128)S(1)}, f32[2,8,256]{2,1,0:T(8,128)S(1)}) custom-call(s32[2,6]{1,0:T(2,128)} %pair_ref.1, s32[1]{0:T(128)S(6)} %copy.7.count_ref, f32[3,512]{1,0:T(4,128)} %position_ref.1, f32[3,512]{1,0:T(4,128)} %strength_ref.1), custom_call_target="tpu_custom_call" | custom-call | tf_op jit(solution)/shard_map/pack/pallas_call | solution.py:306
  2.1 27.2 %all_to_all.20.refs_0_.region_ref = f32[32,1,3200]{2,1,0:T(1,128)S(1)} all-to-all(f32[32,1,3200]{2,1,0:T(1,128)S(1)} %get-tuple-element.10), channel_id=1, replica_groups=mesh['group'=16,'dev'=32] {'dev'}, dimensions={0} | all-to-all | bytes 819200 | tf_op jit(solution)/shard_map/all_to_all | solution.py:372
  29.3 0.8 moments.2
  30.1 10.0 %all-to-all-start.1 = ((f32[16,1,384]{2,1,0:T(1,128)}), f32[16,1,384]{2,1,0:T(1,128)S(1)}, u32[]{:S(2)}, u32[]{:S(2)}) async-start(f32[16,1,384]{2,1,0:T(1,128)} %moments.2), calls=%async_computation.1 | async-start | bytes 49152 | tf_op jit(solution)/shard_map/all_to_all | solution.py:372
  40.1 1.8 %self_terms.2 = (f32[2,32,256]{2,1,0:T(8,128)S(1)}, s32[8,128]{1,0:T(8,128)S(1)}, s32[1,128]{1,0:T(1,128)S(1)}) custom-call(f32[2,8,256]{2,1,0:T(8,128)S(1)} %get-tuple-element.9.mine_ref, f32[32,1,3200]{2,1,0:T(1,128)S(1)} %all_to_all.20.refs_0_.region_ref, s32[2,64]{1,0:T(2,128)} %bitcast.1), custom_call_target="tpu_custom_call" | custom-call | flops 4000000 | bytes 60000 | tf_op jit(solution)/shard_map/self_terms/pallas_call | solution.py:331
  42.0 3.3 %near.2.sum_ref = f32[2,16,256]{2,1,0:T(8,128)S(1)} custom-call(s32[8,128]{1,0:T(8,128)S(1)} %get-tuple-element.13.count_ref, f32[2,32,256]{2,1,0:T(8,128)S(1)} %get-tuple-element.12.self_ref, f32[32,1,3200]{2,1,0:T(1,128)S(1)} %all_to_all.20.refs_0_.region_ref), custom_call_target="tpu_custom_call" | custom-call | flops 20000000 | bytes 600000 | tf_op jit(solution)/shard_map/near/pallas_call | solution.py:343
  45.3 2.2 %all-to-all-done.1.moment_ref = f32[16,1,384]{2,1,0:T(1,128)S(1)} async-done(((f32[16,1,384]{2,1,0:T(1,128)}), f32[16,1,384]{2,1,0:T(1,128)S(1)}, u32[]{:S(2)}, u32[]{:S(2)}) %all-to-all-start.1) | async-done | bytes 24608 | tf_op jit(solution)/shard_map/all_to_all | solution.py:372
  47.5 0.8 far.2
  48.2 18.0 %all_to_all.21.region_ref = f32[32,1,3200]{2,1,0:T(1,128)S(1)} all-to-all(f32[32,1,3200]{2,1,0:T(1,128)S(1)} %get-tuple-element.15), channel_id=1, replica_groups=mesh['group'=16,'dev'=32] {'dev'}, dimensions={0} | all-to-all | bytes 819200 | tf_op jit(solution)/shard_map/all_to_all | solution.py:372
  66.2 0.8 moments.3
  67.0 7.6 %all-to-all-start.3 = ((f32[16,1,384]{2,1,0:T(1,128)}), f32[16,1,384]{2,1,0:T(1,128)S(1)}, u32[]{:S(2)}, u32[]{:S(2)}) async-start(f32[16,1,384]{2,1,0:T(1,128)} %moments.3), calls=%async_computation.3 | async-start | bytes 49152 | tf_op jit(solution)/shard_map/all_to_all | solution.py:372
  74.5 1.0 %self_terms.3.self_ref = f32[2,32,256]{2,1,0:T(8,128)S(1)} custom-call(f32[2,8,256]{2,1,0:T(8,128)S(1)} %get-tuple-element.14.mine_ref), custom_call_target="tpu_custom_call" | custom-call | flops 4000000 | bytes 60000 | tf_op jit(solution)/shard_map/self_terms/pallas_call | solution.py:331
  75.5 3.3 %near.3.sum_ref = f32[2,16,256]{2,1,0:T(8,128)S(1)} custom-call(s32[8,128]{1,0:T(8,128)S(1)} %get-tuple-element.13.count_ref, f32[2,32,256]{2,1,0:T(8,128)S(1)} %self_terms.3.self_ref, f32[32,1,3200]{2,1,0:T(1,128)S(1)} %all_to_all.21.region_ref), custom_call_target="tpu_custom_call" | custom-call | flops 20000000 | bytes 600000 | tf_op jit(solution)/shard_map/near/pallas_call | solution.py:343
  78.8 3.1 %all-to-all-done.3.moment_ref = f32[16,1,384]{2,1,0:T(1,128)S(1)} async-done(((f32[16,1,384]{2,1,0:T(1,128)}), f32[16,1,384]{2,1,0:T(1,128)S(1)}, u32[]{:S(2)}, u32[]{:S(2)}) %all-to-all-start.3) | async-done | bytes 24608 | tf_op jit(solution)/shard_map/all_to_all | solution.py:372
  81.9 1.3 %far.3 = (f32[3,512]{1,0:T(4,128)}, f32[3,512]{1,0:T(4,128)}) custom-call(s32[1,128]{1,0:T(1,128)S(1)} %get-tuple-element.11.far_ref, f32[2,8,256]{2,1,0:T(8,128)S(1)} %get-tuple-element.14.mine_ref, f32[2,32,256]{2,1,0:T(8,128)S(1)} %self_terms.3.self_ref, f32[2,16,256]{2,1,0:T(8,128)S(1)} %near.3.sum_ref, f32[16,1,384]{2,1,0:T(1,128)S(1)} %all-to-all-done.3.moment_ref), custom_call_target="tpu_custom_call" | custom-call | tf_op jit(solution)/shard_map/far/pallas_call | solution.py:361
Async XLA Ops:
  30.1 17.4 %all-to-all-start.1 = ((f32[16,1,384]{2,1,0:T(1,128)}), f32[16,1,384]{2,1,0:T(1,128)S(1)}, u32[]{:S(2)}, u32[]{:S(2)}) async-start(f32[16,1,384]{2,1,0:T(1,128)} %moments.2), calls=%async_computation.1 | async-start | bytes 49152 | tf_op jit(solution)/shard_map/all_to_all | solution.py:372
  67.0 14.9 %all-to-all-start.3 = ((f32[16,1,384]{2,1,0:T(1,128)}), f32[16,1,384]{2,1,0:T(1,128)S(1)}, u32[]{:S(2)}, u32[]{:S(2)}) async-start(f32[16,1,384]{2,1,0:T(1,128)} %moments.3), calls=%async_computation.3 | async-start | bytes 49152 | tf_op jit(solution)/shard_map/all_to_all | solution.py:372

commit v6 on v5

--- a/solution.py
+++ b/solution.py
@@ -130,12 +130,16 @@
 def pack_kernel(pair_ref, count_ref, position_ref, strength_ref, *out_refs):
     zero = jnp.zeros((2, 2 * BS), jnp.float32)
     state = jnp.concatenate([position_ref[...], strength_ref[...], zero], axis=0)
-    lane = lax.broadcasted_iota(jnp.int32, (1, 128), 1)
-    info = jnp.zeros((1, 128), jnp.int32)
-    for side in range(2):
-        for slot in range(6):
-            info = jnp.where(lane == 16 + 6 * side + slot, pair_ref[side, slot], info)
-    info = jnp.where(lane == 28, count_ref[0], info)
+    info = jnp.concatenate(
+        [
+            jnp.zeros((1, 16), jnp.int32),
+            pair_ref[0:1],
+            pair_ref[1:2],
+            count_ref[...],
+            jnp.zeros((1, 99), jnp.int32),
+        ],
+        axis=1,
+    )
     publish([state[:, 0:BS], state[:, BS:]], info.astype(jnp.float32), *out_refs)
 
 
@@ -306,10 +310,10 @@
     return pl.pallas_call(
         pack_kernel,
         out_shape=PUBLISHED,
-        in_specs=in_smem(2) + in_vmem(2),
+        in_specs=in_vmem(4),
         out_specs=tuple(in_vmem(2)),
         name="pack",
-    )(pair_list, pair_count, positions, strengths)
+    )(pair_list, pair_count.reshape(1, 1), positions, strengths)
 
 
 def moments_of(region):

time: 83.5 us -> 83.4 us (level)
  waiting for transfers between devices: 5.25 us -> 6.41 us
  Pallas kernels: 13.8 us -> 12.7 us
    pallas_call x2, Pallas kernels: 6.64 us -> 5.48 us  [near(): pl.pallas_call(near_kernel, out_shape=kept(2, 16, BS), in_specs=in_vmem(3...]
    all_to_all x2, waiting for transfers between devices: 5.25 us -> 6.41 us  [exchange(): return lax.all_to_all(value, axis, 0, 0, tiled=True)]
  transfers between devices with their start and end apart: 2 -> 2, of which waited for: 2 -> 2; matrix products, arithmetic and copies ran while one was open for 0% -> 0% of each run, Pallas kernels for 11% -> 10%
where the time goes in v6:
time: 83.4 us; the launch traced here: 83 us
  blocking collectives  45.2 us (54%)
  starting transfers between devices  17.4 us (21%)
  Pallas kernels  12.7 us (15%)
  waiting for transfers between devices  6.41 us (8%)
  between operations  1.32 us (2%)
    all_to_all x2, blocking collectives, exchange(): return lax.all_to_all(value, axis, 0, 0, tiled=True)  45.2 us
    all_to_all x2, starting transfers between devices, exchange(): return lax.all_to_all(value, axis, 0, 0, tiled=True)  17.4 us
    all_to_all x2, waiting for transfers between devices, exchange(): return lax.all_to_all(value, axis, 0, 0, tiled=True)  6.41 us
    pallas_call x2, Pallas kernels, near(): pl.pallas_call(near_kernel, out_shape=kept(2, 16, BS), in_specs=in_vmem(3...  5.48 us
    pallas_call x2, Pallas kernels, self_terms(): pl.pallas_call(self_kernel, out_shape=out_shape, in_specs=in_specs, out_s...  2.78 us
    pallas_call x2, Pallas kernels, far(): pl.pallas_call(functools.partial(far_kernel, last), out_shape=out_shape,...  2.01 us
  transfers between devices with their start and end apart: 2, of which 2 were waited for; matrix products, arithmetic and copies ran while one was open for 0% of the time, Pallas kernels for 10%

profile of v6, /device:TPU:1, one launch (start us, length us, event | category | flops | bytes accessed | tf_op | source)
XLA Modules:
  0.0 83.0 jit_solution(16696309223502827100)
XLA Ops:
  1.3 0.8 %pack.1 = (f32[32,1,3200]{2,1,0:T(1,128)S(1)}, f32[2,8,256]{2,1,0:T(8,128)S(1)}) custom-call(s32[2,6]{1,0:T(2,128)} %pair_ref.1, s32[1,1]{1,0:T(1,128)} %bitcast.2.count_ref, f32[3,512]{1,0:T(4,128)} %position_ref.1, f32[3,512]{1,0:T(4,128)} %strength_ref.1), custom_call_target="tpu_custom_call" | custom-call | tf_op jit(solution)/shard_map/pack/pallas_call | solution.py:310
  2.1 27.2 %all_to_all.20.refs_0_.region_ref = f32[32,1,3200]{2,1,0:T(1,128)S(1)} all-to-all(f32[32,1,3200]{2,1,0:T(1,128)S(1)} %get-tuple-element.10), channel_id=1, replica_groups=mesh['group'=16,'dev'=32] {'dev'}, dimensions={0} | all-to-all | bytes 819200 | tf_op jit(solution)/shard_map/all_to_all | solution.py:376
  29.3 0.8 moments.2
  30.1 10.0 %all-to-all-start.1 = ((f32[16,1,384]{2,1,0:T(1,128)}), f32[16,1,384]{2,1,0:T(1,128)S(1)}, u32[]{:S(2)}, u32[]{:S(2)}) async-start(f32[16,1,384]{2,1,0:T(1,128)} %moments.2), calls=%async_computation.1 | async-start | bytes 49152 | tf_op jit(solution)/shard_map/all_to_all | solution.py:376
  40.2 1.8 %self_terms.2 = (f32[2,32,256]{2,1,0:T(8,128)S(1)}, s32[8,128]{1,0:T(8,128)S(1)}, s32[1,128]{1,0:T(1,128)S(1)}) custom-call(f32[2,8,256]{2,1,0:T(8,128)S(1)} %get-tuple-element.9.mine_ref, f32[32,1,3200]{2,1,0:T(1,128)S(1)} %all_to_all.20.refs_0_.region_ref, s32[2,64]{1,0:T(2,128)} %bitcast.3), custom_call_target="tpu_custom_call" | custom-call | flops 4000000 | bytes 60000 | tf_op jit(solution)/shard_map/self_terms/pallas_call | solution.py:335
  42.0 2.7 %near.2.sum_ref = f32[2,16,256]{2,1,0:T(8,128)S(1)} custom-call(s32[8,128]{1,0:T(8,128)S(1)} %get-tuple-element.13.count_ref, f32[2,32,256]{2,1,0:T(8,128)S(1)} %get-tuple-element.12.self_ref, f32[32,1,3200]{2,1,0:T(1,128)S(1)} %all_to_all.20.refs_0_.region_ref), custom_call_target="tpu_custom_call" | custom-call | flops 20000000 | bytes 600000 | tf_op jit(solution)/shard_map/near/pallas_call | solution.py:347
  44.7 2.8 %all-to-all-done.1.moment_ref = f32[16,1,384]{2,1,0:T(1,128)S(1)} async-done(((f32[16,1,384]{2,1,0:T(1,128)}), f32[16,1,384]{2,1,0:T(1,128)S(1)}, u32[]{:S(2)}, u32[]{:S(2)}) %all-to-all-start.1) | async-done | bytes 24608 | tf_op jit(solution)/shard_map/all_to_all | solution.py:376
  47.5 0.8 far.2
  48.3 18.0 %all_to_all.21.region_ref = f32[32,1,3200]{2,1,0:T(1,128)S(1)} all-to-all(f32[32,1,3200]{2,1,0:T(1,128)S(1)} %get-tuple-element.15), channel_id=1, replica_groups=mesh['group'=16,'dev'=32] {'dev'}, dimensions={0} | all-to-all | bytes 819200 | tf_op jit(solution)/shard_map/all_to_all | solution.py:376
  66.2 0.8 moments.3
  67.0 7.4 %all-to-all-start.3 = ((f32[16,1,384]{2,1,0:T(1,128)}), f32[16,1,384]{2,1,0:T(1,128)S(1)}, u32[]{:S(2)}, u32[]{:S(2)}) async-start(f32[16,1,384]{2,1,0:T(1,128)} %moments.3), calls=%async_computation.3 | async-start | bytes 49152 | tf_op jit(solution)/shard_map/all_to_all | solution.py:376
  74.4 1.0 %self_terms.3.self_ref = f32[2,32,256]{2,1,0:T(8,128)S(1)} custom-call(f32[2,8,256]{2,1,0:T(8,128)S(1)} %get-tuple-element.14.mine_ref), custom_call_target="tpu_custom_call" | custom-call | flops 4000000 | bytes 60000 | tf_op jit(solution)/shard_map/self_terms/pallas_call | solution.py:335
  75.3 2.7 %near.3.sum_ref = f32[2,16,256]{2,1,0:T(8,128)S(1)} custom-call(s32[8,128]{1,0:T(8,128)S(1)} %get-tuple-element.13.count_ref, f32[2,32,256]{2,1,0:T(8,128)S(1)} %self_terms.3.self_ref, f32[32,1,3200]{2,1,0:T(1,128)S(1)} %all_to_all.21.region_ref), custom_call_target="tpu_custom_call" | custom-call | flops 20000000 | bytes 600000 | tf_op jit(solution)/shard_map/near/pallas_call | solution.py:347
  78.1 3.6 %all-to-all-done.3.moment_ref = f32[16,1,384]{2,1,0:T(1,128)S(1)} async-done(((f32[16,1,384]{2,1,0:T(1,128)}), f32[16,1,384]{2,1,0:T(1,128)S(1)}, u32[]{:S(2)}, u32[]{:S(2)}) %all-to-all-start.3) | async-done | bytes 24608 | tf_op jit(solution)/shard_map/all_to_all | solution.py:376
  81.7 1.3 %far.3 = (f32[3,512]{1,0:T(4,128)}, f32[3,512]{1,0:T(4,128)}) custom-call(s32[1,128]{1,0:T(1,128)S(1)} %get-tuple-element.11.far_ref, f32[2,8,256]{2,1,0:T(8,128)S(1)} %get-tuple-element.14.mine_ref, f32[2,32,256]{2,1,0:T(8,128)S(1)} %self_terms.3.self_ref, f32[2,16,256]{2,1,0:T(8,128)S(1)} %near.3.sum_ref, f32[16,1,384]{2,1,0:T(1,128)S(1)} %all-to-all-done.3.moment_ref), custom_call_target="tpu_custom_call" | custom-call | tf_op jit(solution)/shard_map/far/pallas_call | solution.py:365
Async XLA Ops:
  30.1 17.4 %all-to-all-start.1 = ((f32[16,1,384]{2,1,0:T(1,128)}), f32[16,1,384]{2,1,0:T(1,128)S(1)}, u32[]{:S(2)}, u32[]{:S(2)}) async-start(f32[16,1,384]{2,1,0:T(1,128)} %moments.2), calls=%async_computation.1 | async-start | bytes 49152 | tf_op jit(solution)/shard_map/all_to_all | solution.py:376
  67.0 14.7 %all-to-all-start.3 = ((f32[16,1,384]{2,1,0:T(1,128)}), f32[16,1,384]{2,1,0:T(1,128)S(1)}, u32[]{:S(2)}, u32[]{:S(2)}) async-start(f32[16,1,384]{2,1,0:T(1,128)} %moments.3), calls=%async_computation.3 | async-start | bytes 49152 | tf_op jit(solution)/shard_map/all_to_all | solution.py:376

commit v7 on v3

--- a/solution.py
+++ b/solution.py
@@ -31,10 +31,9 @@
     return jnp.concatenate(parts, axis=0).astype(jnp.bfloat16)
 
 
-def fill_kernels(target, source, mats, count):
+def fill_kernels(target, columns, mats, count):
     tx, ty, tz = target[0:1], target[1:2], target[2:3]
     ax, ay, az = target[3:4], target[4:5], target[5:6]
-    columns = source.T
     for start in range(0, count, CHUNK):
         part = columns[start : start + CHUNK]
         dx = tx - part[:, 0:1]
@@ -181,7 +180,7 @@
         state = mine_ref[block]
         centre = centre_of(state)
         target = state - centre
-        fill_kernels(target, target, mats.at[block], BS)
+        fill_kernels(target, target.T, mats.at[block], BS)
         out_ref[block, 0:16] = weighted_sums(target, mats.at[block], BS)
         out_ref[block, 16:24] = target
         out_ref[block, 24:32] = centre
@@ -215,7 +214,7 @@
             rows.append(region_ref[source >> 1, :, lanes])
         rows.append(jnp.zeros((2, BS), jnp.float32))
         rows = jnp.concatenate(rows, axis=0) - self_ref[block, 24:32]
-        fill_kernels(self_ref[block, 16:24], rows, mats.at[slot], BS)
+        fill_kernels(self_ref[block, 16:24], rows.T, mats.at[slot], BS)
         return block, times * weighted_sums(rows, mats.at[slot], BS)
 
     def visit_two(index, carry):
@@ -260,12 +259,14 @@
 
 def far_kernel(last, far_ref, mine_ref, self_ref, sum_ref, moment_ref, *refs):
     *outs, mats = refs
-    rows = far_sources(far_ref, moment_ref)
+    centres = [self_ref[block, 24:32][:, 0:64] for block in range(2)]
+    rows = far_sources(far_ref, moment_ref) - jnp.concatenate(centres, axis=1)
+    columns = rows.T
     blocks = []
     for block in range(2):
         target = self_ref[block, 16:24]
-        source = rows[:, 64 * block : 64 * block + 64] - self_ref[block, 24:32][:, 0:64]
-        fill_kernels(target, source, mats.at[block], 64)
+        source = rows[:, 64 * block : 64 * block + 64]
+        fill_kernels(target, columns[64 * block : 64 * block + 64], mats.at[block], 64)
         sums = sum_ref[block] + weighted_sums(source, mats.at[block], 64)
         new = mine_ref[block, 0:6] + advance_rows(target, sums)
         blocks.append(jnp.concatenate([new, jnp.zeros((2, BS), jnp.float32)], axis=0))

time: 83.5 us -> 83.6 us (level)
  transfers between devices with their start and end apart: 2 -> 2, of which waited for: 2 -> 2; matrix products, arithmetic and copies ran while one was open for 0% -> 0% of each run, Pallas kernels for 8% -> 9%
where the time goes in v7:
time: 83.6 us; the launch traced here: 83.2 us
  blocking collectives  45.2 us (54%)
  starting transfers between devices  17.5 us (21%)
  Pallas kernels  12.1 us (14%)
  waiting for transfers between devices  7.09 us (8%)
  between operations  1.32 us (2%)
    all_to_all x2, blocking collectives, exchange(): return lax.all_to_all(value, axis, 0, 0, tiled=True)  45.2 us
    all_to_all x2, starting transfers between devices, exchange(): return lax.all_to_all(value, axis, 0, 0, tiled=True)  17.5 us
    all_to_all x2, waiting for transfers between devices, exchange(): return lax.all_to_all(value, axis, 0, 0, tiled=True)  7.09 us
    pallas_call x2, Pallas kernels, near(): pl.pallas_call(near_kernel, out_shape=kept(2, 16, BS), in_specs=in_vmem(3...  5.47 us
    pallas_call x2, Pallas kernels, self_terms(): pl.pallas_call(self_kernel, out_shape=out_shape, in_specs=in_specs, out_s...  2.1 us
    pallas_call x2, Pallas kernels, far(): pl.pallas_call(functools.partial(far_kernel, last), out_shape=out_shape,...  2.01 us
  transfers between devices with their start and end apart: 2, of which 2 were waited for; matrix products, arithmetic and copies ran while one was open for 0% of the time, Pallas kernels for 9%

profile of v7, /device:TPU:1, one launch (start us, length us, event | category | flops | bytes accessed | tf_op | source)
XLA Modules:
  0.0 83.2 jit_solution(18345544316562702229)
XLA Ops:
  1.3 0.9 %pack.1 = (s32[1,128]{1,0:T(1,128)S(1)}, f32[32,1,3200]{2,1,0:T(1,128)S(1)}, f32[2,8,256]{2,1,0:T(8,128)S(1)}) custom-call(s32[2,6]{1,0:T(2,128)} %pair_ref.1, s32[1]{0:T(128)S(6)} %copy.7.count_ref, f32[3,512]{1,0:T(4,128)} %position_ref.1, f32[3,512]{1,0:T(4,128)} %strength_ref.1, s32[2,64]{1,0:T(2,128)} %bitcast.1), custom_call_target="tpu_custom_call" | custom-call | tf_op jit(solution)/shard_map/pack/pallas_call | solution.py:306
  2.2 27.2 %all_to_all.20.refs_0_.region_ref = f32[32,1,3200]{2,1,0:T(1,128)S(1)} all-to-all(f32[32,1,3200]{2,1,0:T(1,128)S(1)} %get-tuple-element.11), channel_id=1, replica_groups=mesh['group'=16,'dev'=32] {'dev'}, dimensions={0} | all-to-all | bytes 819200 | tf_op jit(solution)/shard_map/all_to_all | solution.py:372
  29.4 0.8 moments.2
  30.2 10.0 %all-to-all-start.1 = ((f32[16,1,384]{2,1,0:T(1,128)}), f32[16,1,384]{2,1,0:T(1,128)S(1)}, u32[]{:S(2)}, u32[]{:S(2)}) async-start(f32[16,1,384]{2,1,0:T(1,128)} %moments.2), calls=%async_computation.1 | async-start | bytes 49152 | tf_op jit(solution)/shard_map/all_to_all | solution.py:372
  40.2 1.1 %self_terms.2 = (f32[2,32,256]{2,1,0:T(8,128)S(1)}, s32[8,128]{1,0:T(8,128)S(1)}) custom-call(f32[2,8,256]{2,1,0:T(8,128)S(1)} %get-tuple-element.10.mine_ref, f32[32,1,3200]{2,1,0:T(1,128)S(1)} %all_to_all.20.refs_0_.region_ref), custom_call_target="tpu_custom_call" | custom-call | flops 4000000 | bytes 60000 | tf_op jit(solution)/shard_map/self_terms/pallas_call | solution.py:331
  41.4 2.7 %near.2.sum_ref = f32[2,16,256]{2,1,0:T(8,128)S(1)} custom-call(s32[8,128]{1,0:T(8,128)S(1)} %get-tuple-element.13.count_ref, f32[2,32,256]{2,1,0:T(8,128)S(1)} %get-tuple-element.12.self_ref, f32[32,1,3200]{2,1,0:T(1,128)S(1)} %all_to_all.20.refs_0_.region_ref), custom_call_target="tpu_custom_call" | custom-call | flops 20000000 | bytes 600000 | tf_op jit(solution)/shard_map/near/pallas_call | solution.py:343
  44.1 3.4 %all-to-all-done.1.moment_ref = f32[16,1,384]{2,1,0:T(1,128)S(1)} async-done(((f32[16,1,384]{2,1,0:T(1,128)}), f32[16,1,384]{2,1,0:T(1,128)S(1)}, u32[]{:S(2)}, u32[]{:S(2)}) %all-to-all-start.1) | async-done | bytes 24608 | tf_op jit(solution)/shard_map/all_to_all | solution.py:372
  47.6 0.8 far.2
  48.4 18.0 %all_to_all.21.region_ref = f32[32,1,3200]{2,1,0:T(1,128)S(1)} all-to-all(f32[32,1,3200]{2,1,0:T(1,128)S(1)} %get-tuple-element.15), channel_id=1, replica_groups=mesh['group'=16,'dev'=32] {'dev'}, dimensions={0} | all-to-all | bytes 819200 | tf_op jit(solution)/shard_map/all_to_all | solution.py:372
  66.3 0.8 moments.3
  67.1 7.5 %all-to-all-start.3 = ((f32[16,1,384]{2,1,0:T(1,128)}), f32[16,1,384]{2,1,0:T(1,128)S(1)}, u32[]{:S(2)}, u32[]{:S(2)}) async-start(f32[16,1,384]{2,1,0:T(1,128)} %moments.3), calls=%async_computation.3 | async-start | bytes 49152 | tf_op jit(solution)/shard_map/all_to_all | solution.py:372
  74.6 1.0 %self_terms.3.self_ref = f32[2,32,256]{2,1,0:T(8,128)S(1)} custom-call(f32[2,8,256]{2,1,0:T(8,128)S(1)} %get-tuple-element.14.mine_ref), custom_call_target="tpu_custom_call" | custom-call | flops 4000000 | bytes 60000 | tf_op jit(solution)/shard_map/self_terms/pallas_call | solution.py:331
  75.5 2.7 %near.3.sum_ref = f32[2,16,256]{2,1,0:T(8,128)S(1)} custom-call(s32[8,128]{1,0:T(8,128)S(1)} %get-tuple-element.13.count_ref, f32[2,32,256]{2,1,0:T(8,128)S(1)} %self_terms.3.self_ref, f32[32,1,3200]{2,1,0:T(1,128)S(1)} %all_to_all.21.region_ref), custom_call_target="tpu_custom_call" | custom-call | flops 20000000 | bytes 600000 | tf_op jit(solution)/shard_map/near/pallas_call | solution.py:343
  78.3 3.6 %all-to-all-done.3.moment_ref = f32[16,1,384]{2,1,0:T(1,128)S(1)} async-done(((f32[16,1,384]{2,1,0:T(1,128)}), f32[16,1,384]{2,1,0:T(1,128)S(1)}, u32[]{:S(2)}, u32[]{:S(2)}) %all-to-all-start.3) | async-done | bytes 24608 | tf_op jit(solution)/shard_map/all_to_all | solution.py:372
  81.9 1.3 %far.3 = (f32[3,512]{1,0:T(4,128)}, f32[3,512]{1,0:T(4,128)}) custom-call(s32[1,128]{1,0:T(1,128)S(1)} %get-tuple-element.9.far_ref, f32[2,8,256]{2,1,0:T(8,128)S(1)} %get-tuple-element.14.mine_ref, f32[2,32,256]{2,1,0:T(8,128)S(1)} %self_terms.3.self_ref, f32[2,16,256]{2,1,0:T(8,128)S(1)} %near.3.sum_ref, f32[16,1,384]{2,1,0:T(1,128)S(1)} %all-to-all-done.3.moment_ref), custom_call_target="tpu_custom_call" | custom-call | tf_op jit(solution)/shard_map/far/pallas_call | solution.py:361
Async XLA Ops:
  30.2 17.4 %all-to-all-start.1 = ((f32[16,1,384]{2,1,0:T(1,128)}), f32[16,1,384]{2,1,0:T(1,128)S(1)}, u32[]{:S(2)}, u32[]{:S(2)}) async-start(f32[16,1,384]{2,1,0:T(1,128)} %moments.2), calls=%async_computation.1 | async-start | bytes 49152 | tf_op jit(solution)/shard_map/all_to_all | solution.py:372
  67.1 14.8 %all-to-all-start.3 = ((f32[16,1,384]{2,1,0:T(1,128)}), f32[16,1,384]{2,1,0:T(1,128)S(1)}, u32[]{:S(2)}, u32[]{:S(2)}) async-start(f32[16,1,384]{2,1,0:T(1,128)} %moments.3), calls=%async_computation.3 | async-start | bytes 49152 | tf_op jit(solution)/shard_map/all_to_all | solution.py:372

commit v8 on v7

--- a/solution.py
+++ b/solution.py
@@ -13,7 +13,7 @@
 N_DEV = NZ * NX
 N_GROUP = NY * NC
 REGION_BLOCKS = 2 * N_DEV
-CHUNK = 32
+CHUNK = 64
 
 INV_FOUR_PI = 0.07957747154594767
 CORE_SQUARED = 0.25

time: 83.6 us -> 82.9 us (level)
  Pallas kernels: 12.1 us -> 15.7 us
  waiting for transfers between devices: 7.09 us -> 3.51 us
    pallas_call x2, Pallas kernels: 5.47 us -> 9.06 us  [near(): pl.pallas_call(near_kernel, out_shape=kept(2, 16, BS), in_specs=in_vmem(3...]
    all_to_all x2, waiting for transfers between devices: 7.09 us -> 3.51 us  [exchange(): return lax.all_to_all(value, axis, 0, 0, tiled=True)]
  transfers between devices with their start and end apart: 2 -> 2, of which waited for: 2 -> 2; matrix products, arithmetic and copies ran while one was open for 0% -> 0% of each run, Pallas kernels for 9% -> 13%
where the time goes in v8:
time: 82.9 us; the launch traced here: 82.6 us
  blocking collectives  45.2 us (55%)
  starting transfers between devices  16.9 us (20%)
  Pallas kernels  15.7 us (19%)
  waiting for transfers between devices  3.51 us (4%)
  between operations  1.32 us (2%)
    all_to_all x2, blocking collectives, exchange(): return lax.all_to_all(value, axis, 0, 0, tiled=True)  45.2 us
    all_to_all x2, starting transfers between devices, exchange(): return lax.all_to_all(value, axis, 0, 0, tiled=True)  16.9 us
    pallas_call x2, Pallas kernels, near(): pl.pallas_call(near_kernel, out_shape=kept(2, 16, BS), in_specs=in_vmem(3...  9.06 us
    all_to_all x2, waiting for transfers between devices, exchange(): return lax.all_to_all(value, axis, 0, 0, tiled=True)  3.51 us
    pallas_call x2, Pallas kernels, self_terms(): pl.pallas_call(self_kernel, out_shape=out_shape, in_specs=in_specs, out_s...  2.09 us
    pallas_call x2, Pallas kernels, far(): pl.pallas_call(functools.partial(far_kernel, last), out_shape=out_shape,...  2.02 us
  transfers between devices with their start and end apart: 2, of which 2 were waited for; matrix products, arithmetic and copies ran while one was open for 0% of the time, Pallas kernels for 13%

profile of v8, /device:TPU:1, one launch (start us, length us, event | category | flops | bytes accessed | tf_op | source)
XLA Modules:
  0.0 82.6 jit_solution(16119207521341458063)
XLA Ops:
  1.3 0.9 %pack.1 = (s32[1,128]{1,0:T(1,128)S(1)}, f32[32,1,3200]{2,1,0:T(1,128)S(1)}, f32[2,8,256]{2,1,0:T(8,128)S(1)}) custom-call(s32[2,6]{1,0:T(2,128)} %pair_ref.1, s32[1]{0:T(128)S(6)} %copy.7.count_ref, f32[3,512]{1,0:T(4,128)} %position_ref.1, f32[3,512]{1,0:T(4,128)} %strength_ref.1, s32[2,64]{1,0:T(2,128)} %bitcast.1), custom_call_target="tpu_custom_call" | custom-call | tf_op jit(solution)/shard_map/pack/pallas_call | solution.py:306
  2.2 27.2 %all_to_all.20.refs_0_.region_ref = f32[32,1,3200]{2,1,0:T(1,128)S(1)} all-to-all(f32[32,1,3200]{2,1,0:T(1,128)S(1)} %get-tuple-element.11), channel_id=1, replica_groups=mesh['group'=16,'dev'=32] {'dev'}, dimensions={0} | all-to-all | bytes 819200 | tf_op jit(solution)/shard_map/all_to_all | solution.py:372
  29.4 0.8 moments.2
  30.2 10.0 %all-to-all-start.1 = ((f32[16,1,384]{2,1,0:T(1,128)}), f32[16,1,384]{2,1,0:T(1,128)S(1)}, u32[]{:S(2)}, u32[]{:S(2)}) async-start(f32[16,1,384]{2,1,0:T(1,128)} %moments.2), calls=%async_computation.1 | async-start | bytes 49152 | tf_op jit(solution)/shard_map/all_to_all | solution.py:372
  40.2 1.1 %self_terms.2 = (f32[2,32,256]{2,1,0:T(8,128)S(1)}, s32[8,128]{1,0:T(8,128)S(1)}) custom-call(f32[2,8,256]{2,1,0:T(8,128)S(1)} %get-tuple-element.10.mine_ref, f32[32,1,3200]{2,1,0:T(1,128)S(1)} %all_to_all.20.refs_0_.region_ref), custom_call_target="tpu_custom_call" | custom-call | flops 4000000 | bytes 60000 | tf_op jit(solution)/shard_map/self_terms/pallas_call | solution.py:331
  41.4 4.5 %near.2.sum_ref = f32[2,16,256]{2,1,0:T(8,128)S(1)} custom-call(s32[8,128]{1,0:T(8,128)S(1)} %get-tuple-element.13.count_ref, f32[2,32,256]{2,1,0:T(8,128)S(1)} %get-tuple-element.12.self_ref, f32[32,1,3200]{2,1,0:T(1,128)S(1)} %all_to_all.20.refs_0_.region_ref), custom_call_target="tpu_custom_call" | custom-call | flops 20000000 | bytes 600000 | tf_op jit(solution)/shard_map/near/pallas_call | solution.py:343
  45.9 1.7 %all-to-all-done.1.moment_ref = f32[16,1,384]{2,1,0:T(1,128)S(1)} async-done(((f32[16,1,384]{2,1,0:T(1,128)}), f32[16,1,384]{2,1,0:T(1,128)S(1)}, u32[]{:S(2)}, u32[]{:S(2)}) %all-to-all-start.1) | async-done | bytes 24608 | tf_op jit(solution)/shard_map/all_to_all | solution.py:372
  47.6 0.8 far.2
  48.4 18.0 %all_to_all.21.region_ref = f32[32,1,3200]{2,1,0:T(1,128)S(1)} all-to-all(f32[32,1,3200]{2,1,0:T(1,128)S(1)} %get-tuple-element.15), channel_id=1, replica_groups=mesh['group'=16,'dev'=32] {'dev'}, dimensions={0} | all-to-all | bytes 819200 | tf_op jit(solution)/shard_map/all_to_all | solution.py:372
  66.3 0.8 moments.3
  67.1 6.9 %all-to-all-start.3 = ((f32[16,1,384]{2,1,0:T(1,128)}), f32[16,1,384]{2,1,0:T(1,128)S(1)}, u32[]{:S(2)}, u32[]{:S(2)}) async-start(f32[16,1,384]{2,1,0:T(1,128)} %moments.3), calls=%async_computation.3 | async-start | bytes 49152 | tf_op jit(solution)/shard_map/all_to_all | solution.py:372
  74.0 1.0 %self_terms.3.self_ref = f32[2,32,256]{2,1,0:T(8,128)S(1)} custom-call(f32[2,8,256]{2,1,0:T(8,128)S(1)} %get-tuple-element.14.mine_ref), custom_call_target="tpu_custom_call" | custom-call | flops 4000000 | bytes 60000 | tf_op jit(solution)/shard_map/self_terms/pallas_call | solution.py:331
  74.9 4.5 %near.3.sum_ref = f32[2,16,256]{2,1,0:T(8,128)S(1)} custom-call(s32[8,128]{1,0:T(8,128)S(1)} %get-tuple-element.13.count_ref, f32[2,32,256]{2,1,0:T(8,128)S(1)} %self_terms.3.self_ref, f32[32,1,3200]{2,1,0:T(1,128)S(1)} %all_to_all.21.region_ref), custom_call_target="tpu_custom_call" | custom-call | flops 20000000 | bytes 600000 | tf_op jit(solution)/shard_map/near/pallas_call | solution.py:343
  79.5 1.9 %all-to-all-done.3.moment_ref = f32[16,1,384]{2,1,0:T(1,128)S(1)} async-done(((f32[16,1,384]{2,1,0:T(1,128)}), f32[16,1,384]{2,1,0:T(1,128)S(1)}, u32[]{:S(2)}, u32[]{:S(2)}) %all-to-all-start.3) | async-done | bytes 24608 | tf_op jit(solution)/shard_map/all_to_all | solution.py:372
  81.3 1.3 %far.3 = (f32[3,512]{1,0:T(4,128)}, f32[3,512]{1,0:T(4,128)}) custom-call(s32[1,128]{1,0:T(1,128)S(1)} %get-tuple-element.9.far_ref, f32[2,8,256]{2,1,0:T(8,128)S(1)} %get-tuple-element.14.mine_ref, f32[2,32,256]{2,1,0:T(8,128)S(1)} %self_terms.3.self_ref, f32[2,16,256]{2,1,0:T(8,128)S(1)} %near.3.sum_ref, f32[16,1,384]{2,1,0:T(1,128)S(1)} %all-to-all-done.3.moment_ref), custom_call_target="tpu_custom_call" | custom-call | tf_op jit(solution)/shard_map/far/pallas_call | solution.py:361
Async XLA Ops:
  30.2 17.4 %all-to-all-start.1 = ((f32[16,1,384]{2,1,0:T(1,128)}), f32[16,1,384]{2,1,0:T(1,128)S(1)}, u32[]{:S(2)}, u32[]{:S(2)}) async-start(f32[16,1,384]{2,1,0:T(1,128)} %moments.2), calls=%async_computation.1 | async-start | bytes 49152 | tf_op jit(solution)/shard_map/all_to_all | solution.py:372
  67.1 14.3 %all-to-all-start.3 = ((f32[16,1,384]{2,1,0:T(1,128)}), f32[16,1,384]{2,1,0:T(1,128)S(1)}, u32[]{:S(2)}, u32[]{:S(2)}) async-start(f32[16,1,384]{2,1,0:T(1,128)} %moments.3), calls=%async_computation.3 | async-start | bytes 49152 | tf_op jit(solution)/shard_map/all_to_all | solution.py:372
